TPU v7x, 512 devices: a whole 4x8x8 slice. The times are simulated.
512 devices in a mesh: pool: 64 (over y_lo, z, core), tensor: 8 (over y_hi, x).
Axes of the slice: x: 4, y: 8 (y_hi: 2, y_lo: 4; y = y_hi * 4 + y_lo), z: 8, core: 2. Of those that a mesh axis runs over, the one named last changes fastest.
Arguments:
- queries: bfloat16 [2, 1024, 8192], P(None, 'pool', 'tensor'), may hold values from -160 to 160
- new_keys: bfloat16 [2, 1024, 1024], P(None, 'pool', 'tensor'), may hold values from -10 to 10
- new_values: bfloat16 [2, 1024, 1024], P(None, 'pool', 'tensor'), may hold values from -6 to 6
- cache_keys: bfloat16 [1024, 128, 1024], P('pool', None, 'tensor'), may hold values from -5 to 5
- cache_values: bfloat16 [1024, 128, 1024], P('pool', None, 'tensor'), may hold values from -6 to 6
- cache_lengths: int32 [1024], P('pool'), may hold values from 2 to 128
- handoff_kv: bfloat16 [64, 48, 8, 2, 1024], P('pool', None, 'tensor'), may hold values from -6 to 6
- page_owner: int32 [3072], replicated, may hold values from 0 to 63, as said below
- page_request: int32 [3072], replicated, may hold values from 0 to 1
- page_length: int32 [3072], replicated, may hold values from 1 to 8
Outputs:
- attended: bfloat16 [2, 1024, 8192], P(None, 'pool', 'tensor')
Inputs may be any that keep to these rules, and one draw needn't show every extreme that they name: `page_owner`: no source instance hands more than 2 pages to one decode instance.
All inputs are finite; a program needn't handle non-finite values.
Results may differ from a plain program's by a relative error of at most 0.0021.
Values may be sent and summed in bfloat16 or wider, within the bound.
No kernel may reach another device: no remote copies, remote signals or barrier semaphores. Data moves between devices by JAX's collectives and lax.ppermute only.
A program may use at most 64 MiB of HBM per device.

v0:
```python
import jax
import jax.numpy as jnp
from jax import lax
from jax.sharding import PartitionSpec as P

HEADS = 64
KV_HEADS = 8
HEAD_DIM = 128
SAMPLES = 8


MASKED_SCORE = -1e30


def page_slots(owner_table):
    page_count = owner_table.shape[1]
    same_owner = owner_table[:, :, None] == owner_table[:, None, :]
    position = jnp.arange(page_count, dtype=jnp.int32)
    before = position[None, :] < position[:, None]
    return jnp.sum(jnp.where(same_owner & before[None], 1, 0), axis=2).astype(jnp.int32)


def body(
    queries,
    new_keys,
    new_values,
    cache_keys,
    cache_values,
    cache_lengths,
    handoff_kv,
    page_owner,
    page_request,
    page_length,
):
    pool_size = lax.axis_size("pool")
    own_index = lax.axis_index("pool")
    pages_dev = handoff_kv.shape[1]
    capacity = max(2, (2 * pages_dev + pool_size - 1) // pool_size)
    owner_table = page_owner.reshape(pool_size, pages_dev)
    slot_table = page_slots(owner_table)
    my_owner = lax.dynamic_index_in_dim(owner_table, own_index, 0, keepdims=False)
    my_slot = lax.dynamic_index_in_dim(slot_table, own_index, 0, keepdims=False)
    slot_ids = jnp.arange(pool_size * capacity, dtype=jnp.int32)
    chosen_slot = (my_owner[None, :] == (slot_ids // capacity)[:, None]) & (
        my_slot[None, :] == (slot_ids % capacity)[:, None]
    )
    source_page = jnp.sum(
        jnp.where(chosen_slot, jnp.arange(pages_dev, dtype=jnp.int32)[None, :], 0), axis=1
    )
    filled = jnp.any(chosen_slot, axis=1)
    page_rows = handoff_kv[0]
    chosen = jnp.take(page_rows, source_page, axis=0)
    chosen = jnp.where(
        filled.reshape((-1,) + (1,) * (page_rows.ndim - 1)), chosen, jnp.zeros((), page_rows.dtype)
    )
    arrived = lax.all_to_all(
        chosen.reshape((pool_size, capacity) + page_rows.shape[1:]),
        "pool",
        split_axis=0,
        concat_axis=0,
        tiled=True,
    )
    received = lax.all_to_all(arrived, "tensor", split_axis=4, concat_axis=2, tiled=True)
    request_table = page_request.reshape(pool_size, pages_dev)
    length_table = page_length.reshape(pool_size, pages_dev)
    cap_ids = jnp.arange(capacity, dtype=jnp.int32)
    matched = (owner_table[:, None, :] == own_index) & (
        slot_table[:, None, :] == cap_ids[None, :, None]
    )
    slot_request = jnp.sum(jnp.where(matched, request_table[:, None, :], 0), axis=2)
    slot_length = jnp.sum(jnp.where(matched, length_table[:, None, :], 0), axis=2)
    head_dim = HEAD_DIM
    group = HEADS // KV_HEADS
    score_scale = HEAD_DIM ** (-0.5)
    row_count = queries.shape[1]
    kv_dev = new_keys.shape[2] // head_dim
    page_len = received.shape[2]
    key_total = pool_size * capacity * page_len
    token_ids = jnp.arange(page_len, dtype=jnp.int32)
    live_token = (token_ids[None, None, :] < slot_length[:, :, None]).reshape(key_total)
    token_request = jnp.broadcast_to(
        slot_request[:, :, None], (pool_size, capacity, page_len)
    ).reshape(key_total)
    row_request = jnp.arange(row_count, dtype=jnp.int32) // SAMPLES
    recv_mask = (row_request[:, None] == token_request[None, :]) & live_token[None, :]
    res_mask = jnp.arange(cache_keys.shape[1], dtype=jnp.int32)[None, :] < cache_lengths[:, None]
    recv_keys = received[:, :, :, 0, :].reshape(key_total, kv_dev * head_dim)
    recv_values = received[:, :, :, 1, :].reshape(key_total, kv_dev * head_dim)
    outputs = []
    for step_index in range(2):
        query_block = queries[step_index].reshape(row_count, kv_dev, group, head_dim)[:, 0]
        res_score = (
            jnp.einsum("rgd,rtd->rgt", query_block, cache_keys, preferred_element_type=jnp.float32)
            * score_scale
        )
        res_score = jnp.where(res_mask[:, None, :], res_score, MASKED_SCORE)
        flat_query = query_block.reshape(row_count * group, head_dim)
        recv_score = (
            lax.dot_general(
                flat_query, recv_keys, (((1,), (1,)), ((), ())), preferred_element_type=jnp.float32
            )
            * score_scale
        )
        recv_score = jnp.where(
            recv_mask[:, None, :], recv_score.reshape(row_count, group, key_total), MASKED_SCORE
        )
        fresh_score = (
            jnp.einsum(
                "rgd,srd->rgs",
                query_block,
                new_keys[: step_index + 1, :, 0:head_dim],
                preferred_element_type=jnp.float32,
            )
            * score_scale
        )
        peak_score = jnp.maximum(
            jnp.maximum(jnp.max(res_score, axis=-1), jnp.max(recv_score, axis=-1)),
            jnp.max(fresh_score, axis=-1),
        )[..., None]
        res_weight = jnp.exp(res_score - peak_score)
        recv_weight = jnp.exp(recv_score - peak_score)
        fresh_weight = jnp.exp(fresh_score - peak_score)
        denominator = (
            jnp.sum(res_weight, axis=-1)
            + jnp.sum(recv_weight, axis=-1)
            + jnp.sum(fresh_weight, axis=-1)
        )
        weighted = jnp.einsum(
            "rgt,rtd->rgd",
            res_weight.astype(jnp.bfloat16),
            cache_values,
            preferred_element_type=jnp.float32,
        )
        recv_part = jnp.dot(
            recv_weight.astype(jnp.bfloat16).reshape(row_count * group, key_total),
            recv_values,
            preferred_element_type=jnp.float32,
        )
        weighted = weighted + recv_part.reshape(row_count, group, head_dim)
        weighted = weighted + jnp.einsum(
            "rgs,srd->rgd",
            fresh_weight.astype(jnp.bfloat16),
            new_values[: step_index + 1, :, 0:head_dim],
            preferred_element_type=jnp.float32,
        )
        pieces = (weighted / denominator[..., None]).reshape(row_count, group * head_dim)
        outputs.append(pieces)
    return jnp.stack(outputs).astype(jnp.bfloat16)


def solution(mesh):
    return jax.shard_map(
        body,
        mesh=mesh,
        in_specs=(
            P(None, "pool", "tensor"),
            P(None, "pool", "tensor"),
            P(None, "pool", "tensor"),
            P("pool", None, "tensor"),
            P("pool", None, "tensor"),
            P("pool"),
            P("pool", None, "tensor", None, None),
            P(),
            P(),
            P(),
        ),
        out_specs=P(None, "pool", "tensor"),
        check_vma=False,
    )
```

profile of v0, /device:TPU:8, one launch (start us, length us, event | category | flops | bytes accessed | tf_op | source)
XLA Modules:
  0.0 73.1 jit_solution(9199669934870876828)
XLA Ops:
  0.0 0.8 %broadcast_in_dim_reshape.2 = s32[64,48]{1,0:T(8,128)S(1)} reshape(s32[3072]{0:T(1024)} %param.17) | data formatting | bytes 24576 | tf_op jit(solution)/shard_map/broadcast_in_dim;reshape | solution.py:67
  1.0 0.5 select_reduce_fusion
  1.4 0.2 dynamic-slice_reduce_fusion
  1.6 0.1 select_reduce_fusion.3
  1.7 0.1 reduce_sum.97
  1.9 0.1 fusion.32
  2.0 0.1 broadcast_in_dim.141
  2.2 2.6 %gather_fusion = bf16[128,2,1024]{2,1,0:T(2,128)(2,1)S(1)} fusion(bf16[48,2,1024]{2,1,0:T(2,128)(2,1)} %bitcast.73, s32[1024]{0:T(1024)S(1)} %pad_clamp_fusion), kind=kCustom, calls=%fused_computation | custom fusion | bytes 1049088 | tf_op jit(solution)/shard_map/jit(_take)/gather | solution.py:52
  4.8 1.5 %broadcast_select_fusion.1 = bf16[64,2,1,2,1024]{4,3,1,2,0:T(2,128)(2,1)} fusion(pred[64,2]{1,0:T(8,128)(4,1)S(1)} %broadcast_in_dim.141, bf16[64,2,1,2,1024]{4,3,1,2,0:T(2,128)(2,1)S(1)} %bitcast.72, pred[64,2]{1,0:T(8,128)(4,1)S(1)} %compare_and_fusion.1), kind=kLoop, calls=%fused_computation.22 | loop fusion | flops 524288 | bytes 1048832 | tf_op jit(solution)/shard_map/jit(_where)/select_n | solution.py:53
  6.3 14.5 %all-to-all-start = ((bf16[64,2,1,2,1024]{4,3,1,2,0:T(2,128)(2,1)}), bf16[64,2,1,2,1024]{4,3,1,2,0:T(2,128)(2,1)S(1)}, u32[]{:S(2)}, u32[]{:S(2)}) async-start(bf16[64,2,1,2,1024]{4,3,1,2,0:T(2,128)(2,1)} %broadcast_select_fusion.1), calls=%async_computation | async-start | bytes 1048576 | tf_op jit(solution)/shard_map/all_to_all | solution.py:56
  20.8 0.1 copy.36
  21.1 0.1 broadcast_in_dim.137
  21.3 0.1 copy.42
  21.5 0.2 fusion.44
  21.7 0.1 iota_compare_fusion
  21.8 0.5 fusion.45
  22.3 15.4 %all-to-all-done = bf16[64,2,1,2,1024]{4,3,1,2,0:T(2,128)(2,1)S(1)} async-done(((bf16[64,2,1,2,1024]{4,3,1,2,0:T(2,128)(2,1)}), bf16[64,2,1,2,1024]{4,3,1,2,0:T(2,128)(2,1)S(1)}, u32[]{:S(2)}, u32[]{:S(2)}) %all-to-all-start) | async-done | bytes 524320 | tf_op jit(solution)/shard_map/all_to_all | solution.py:56
  37.7 1.0 %copy.43 = bf16[64,2,1,2,1024]{0,3,2,1,4:T(2,128)(2,1)S(1)} copy(bf16[64,2,1,2,1024]{4,3,1,2,0:T(2,128)(2,1)S(1)} %all-to-all-done) | data formatting | bytes 1048576 | tf_op jit(solution)/shard_map/all_to_all | solution.py:56
  38.6 1.5 %reshape.276 = bf16[8,2,16384]{2,1,0:T(2,128)(2,1)} reshape(bf16[1024,2,1,2,64]{4,3,2,1,0:T(2,128)(2,1)S(1)} %bitcast.65) | data formatting | bytes 1048576
  40.1 7.0 %all-to-all-start.1 = ((bf16[8,2,16384]{2,1,0:T(2,128)(2,1)}), bf16[8,2,16384]{2,1,0:T(2,128)(2,1)S(1)}, u32[]{:S(2)}, u32[]{:S(2)}) async-start(bf16[8,2,16384]{2,1,0:T(2,128)(2,1)} %reshape.276), calls=%async_computation.1 | async-start | bytes 1048576 | tf_op jit(solution)/shard_map/all_to_all | solution.py:63
  47.2 0.1 copy.40
  47.3 0.1 broadcast_in_dim.136
  47.4 0.1 eq.97
  47.5 0.1 lt.92
  47.7 0.1 reduce_max.64
  47.8 0.1 reduce_max.65
  47.9 0.1 compare_and_fusion
  48.0 0.1 fusion.39
  48.1 0.5 fusion.47
  48.6 18.0 %all-to-all-done.1 = bf16[8,2,16384]{2,1,0:T(2,128)(2,1)S(1)} async-done(((bf16[8,2,16384]{2,1,0:T(2,128)(2,1)}), bf16[8,2,16384]{2,1,0:T(2,128)(2,1)S(1)}, u32[]{:S(2)}, u32[]{:S(2)}) %all-to-all-start.1) | async-done | bytes 524320 | tf_op jit(solution)/shard_map/all_to_all | solution.py:63
  66.6 0.7 reshape.277
  67.2 1.4 %copy.44 = bf16[64,2,1,2,8,128]{5,4,1,0,3,2:T(8,128)(2,1)S(1)} copy(bf16[64,2,1,2,8,128]{0,3,1,5,4,2:T(2,128)(2,1)S(1)} %bitcast.66) | data formatting | bytes 1048576 | tf_op jit(solution)/shard_map/all_to_all | solution.py:63
  68.7 0.3 fusion.48
  69.0 0.1 reduce_max.59
  69.1 0.1 sub.64
  69.2 0.2 fusion.21
  69.4 0.3 copy-done.1
  69.6 0.3 fusion.28
  69.9 0.3 fusion.46
  70.3 0.1 reduce_max.62
  70.4 0.2 fusion.23
  70.6 0.3 fusion.26
  70.9 0.2 fusion.11
  71.2 0.3 fusion.9
  71.6 0.2 fusion.13
  71.9 0.3 convolution_add_fusion.1
  72.2 0.2 fusion.10
  72.5 0.6 pad_maximum_fusion
  (47 shorter events, 1.0 us)
Async XLA Ops:
  0.0 21.8 %copy-start = (bf16[16,128,128]{2,1,0:T(8,128)(2,1)S(1)}, bf16[16,128,128]{2,1,0:T(8,128)(2,1)}, u32[]{:S(2)}) copy-start(bf16[16,128,128]{2,1,0:T(8,128)(2,1)} %param.13) | copy-start | bytes 1572868
  4.7 16.2 %copy-start.3 = (s32[3072]{0:T(1024)S(1)}, s32[3072]{0:T(1024)}, u32[]{:S(2)}) copy-start(s32[3072]{0:T(1024)} %param.18) | copy-start | bytes 36868
  4.7 16.3 %copy-start.4 = (s32[3072]{0:T(1024)S(1)}, s32[3072]{0:T(1024)}, u32[]{:S(2)}) copy-start(s32[3072]{0:T(1024)} %param.19) | copy-start | bytes 36868
  4.8 16.6 %copy-start.2 = (bf16[2,16,1024]{2,1,0:T(8,128)(2,1)S(1)}, bf16[2,16,1024]{2,1,0:T(8,128)(2,1)}, u32[]{:S(2)}) copy-start(bf16[2,16,1024]{2,1,0:T(8,128)(2,1)} %param.10) | copy-start | bytes 196612
  6.3 15.1 %copy-start.7 = (s32[16]{0:T(128)S(1)}, s32[16]{0:T(128)}, u32[]{:S(2)}) copy-start(s32[16]{0:T(128)} %param.15) | copy-start | bytes 196
  6.3 15.2 %copy-start.6 = (bf16[2,16,128]{2,1,0:T(8,128)(2,1)S(1)}, bf16[2,16,128]{2,1,0:T(8,128)(2,1)}, u32[]{:S(2)}) copy-start(bf16[2,16,128]{2,1,0:T(8,128)(2,1)} %param.11) | copy-start | bytes 24580
  6.3 31.4 %all-to-all-start = ((bf16[64,2,1,2,1024]{4,3,1,2,0:T(2,128)(2,1)}), bf16[64,2,1,2,1024]{4,3,1,2,0:T(2,128)(2,1)S(1)}, u32[]{:S(2)}, u32[]{:S(2)}) async-start(bf16[64,2,1,2,1024]{4,3,1,2,0:T(2,128)(2,1)} %broadcast_select_fusion.1), calls=%async_computation | async-start | bytes 1048576 | tf_op jit(solution)/shard_map/all_to_all | solution.py:56
  40.1 7.7 %copy-start.5 = (bf16[2,16,128]{2,1,0:T(8,128)(2,1)S(1)}, bf16[2,16,128]{2,1,0:T(8,128)(2,1)}, u32[]{:S(2)}) copy-start(bf16[2,16,128]{2,1,0:T(8,128)(2,1)} %param.12) | copy-start | bytes 24580
  40.1 26.4 %all-to-all-start.1 = ((bf16[8,2,16384]{2,1,0:T(2,128)(2,1)}), bf16[8,2,16384]{2,1,0:T(2,128)(2,1)S(1)}, u32[]{:S(2)}, u32[]{:S(2)}) async-start(bf16[8,2,16384]{2,1,0:T(2,128)(2,1)} %reshape.276), calls=%async_computation.1 | async-start | bytes 1048576 | tf_op jit(solution)/shard_map/all_to_all | solution.py:63
  68.6 1.0 %copy-start.1 = (bf16[16,128,128]{2,1,0:T(8,128)(2,1)S(1)}, bf16[16,128,128]{2,1,0:T(8,128)(2,1)}, u32[]{:S(2)}) copy-start(bf16[16,128,128]{2,1,0:T(8,128)(2,1)} %param.14) | copy-start | bytes 1572868
where the time goes:
time: 73.5 us; the launch traced here: 73.1 us
  waiting for transfers between devices  33.4 us (45%)
  starting transfers between devices  21.5 us (29%)
  local copies, waits for them, and re-layouts  10.4 us (14%)
  other arithmetic  4.17 us (6%)
  matrix products  3.26 us (4%)
    all_to_all x1, waiting for transfers between devices, body(): lax.all_to_all(arrived, 'tensor', split_axis=4, concat_axis=2, tiled=True)  18 us
    all_to_all x1, waiting for transfers between devices, body(): lax.all_to_all(chosen.reshape((pool_size, capacity) + page_rows.shape[1:]...  15.4 us
    all_to_all x1, starting transfers between devices, body(): lax.all_to_all(chosen.reshape((pool_size, capacity) + page_rows.shape[1:]...  14.5 us
    all_to_all x1, starting transfers between devices, body(): lax.all_to_all(arrived, 'tensor', split_axis=4, concat_axis=2, tiled=True)  7.01 us
    gather x1, local copies, waits for them, and re-layouts, body(): chosen = jnp.take(page_rows, source_page, axis=0)  2.56 us
    unnamed x20, local copies, waits for them, and re-layouts  2.49 us
    select_n x1, other arithmetic, body(): jnp.where(filled.reshape((-1,) + (1,) * (page_rows.ndim - 1)), chosen, jn...  1.52 us
  transfers between devices with their start and end apart: 2, of which 2 were waited for; matrix products, arithmetic and copies ran while one was open for 4% of the time, Pallas kernels for 0%

commit v1 on v0

v1 whole, which is shorter than its diff:
```python
import jax
import jax.numpy as jnp
from jax import lax
from jax.experimental import pallas as pl
from jax.experimental.pallas import tpu as pltpu
from jax.sharding import PartitionSpec as P

HEADS = 64
KV_HEADS = 8
HEAD_DIM = 128
GROUP = HEADS // KV_HEADS
SAMPLES = 8
POOL = 64
TENSOR = 8
PAGES = 48
CAP = 2
ROWS = 16
RES_LEN = 128
SLOTS = POOL * CAP
QUERIES = 2 * ROWS * GROUP

MASKED_SCORE = -1e30
SCORE_SCALE = HEAD_DIM ** (-0.5) * 1.4426950408889634

VMEM = pl.BlockSpec(memory_space=pltpu.VMEM)
SMEM = pl.BlockSpec(memory_space=pltpu.SMEM)
PARAMS = pltpu.CompilerParams(vmem_limit_bytes=32 * 1024 * 1024)


def iota(shape, axis):
    return lax.broadcasted_iota(jnp.int32, shape, axis)


def pack_kernel(owner_ref, pages_ref, out_ref):
    start = lax.axis_index("pool") * PAGES
    row, lane = start // 128, lax.rem(start, 128)
    shift = lax.rem(128 - lane, 128)
    first = jnp.broadcast_to(owner_ref[pl.ds(row, 1), :], (8, 128))
    second = jnp.broadcast_to(owner_ref[pl.ds(jnp.minimum(row + 1, 23), 1), :], (8, 128))
    lanes = iota((8, 128), 1)
    owners = jnp.where(lanes < 128 - lane, pltpu.roll(first, shift, 1), pltpu.roll(second, shift, 1))
    across = jnp.broadcast_to(owners[0:1].astype(jnp.float32), (128, 128))
    down = across.T
    earlier = iota((128, 128), 0) < iota((128, 128), 1)
    rank = jnp.sum(jnp.where((across == down) & earlier, 1.0, 0.0), axis=0, keepdims=True)
    key = (owners * (2 * CAP)).astype(jnp.float32) + 2.0 * rank
    key = key.astype(jnp.int32)
    target = jnp.where(
        lanes < PAGES, key, jnp.where(lanes < 2 * PAGES, pltpu.roll(key, PAGES, 1) + 1, -1)
    )
    slots = jnp.where(iota((2 * SLOTS, 128), 0) == target[0:1], 1.0, 0.0).astype(jnp.bfloat16)
    new = iota((256, 256), 0)
    old = iota((256, 256), 1)
    wanted = (new & 15) * 16 + (new >> 5) * 2 + ((new >> 4) & 1)
    swap = jnp.where(old == wanted, 1.0, 0.0).astype(jnp.bfloat16)
    turned = [
        jnp.dot(swap, pages_ref[256 * i : 256 * (i + 1), :], preferred_element_type=jnp.float32).astype(
            jnp.bfloat16
        )
        for i in range(3)
    ]
    zeros = jnp.zeros((128 - 2 * PAGES, 128), jnp.bfloat16)
    for head in range(0, KV_HEADS, 2):
        block = jnp.concatenate(
            [
                jnp.concatenate(
                    [turned[i][32 * h + 16 * kv : 32 * h + 16 * kv + 16] for kv in range(2) for i in range(3)]
                    + [zeros],
                    axis=0,
                )
                for h in (head, head + 1)
            ],
            axis=1,
        )
        placed = jnp.dot(slots, block, preferred_element_type=jnp.float32).astype(jnp.bfloat16)
        out_ref[head * 256 : head * 256 + 256, :] = placed[:, 0:128]
        out_ref[head * 256 + 256 : head * 256 + 512, :] = placed[:, 128:256]


def pack(owners, pages):
    return pl.pallas_call(
        pack_kernel,
        out_shape=jax.ShapeDtypeStruct((KV_HEADS * SLOTS * 2, 128), jnp.bfloat16),
        in_specs=[VMEM, VMEM],
        out_specs=VMEM,
        compiler_params=PARAMS,
        name="pack",
    )(owners, pages)


def resident_kernel(len_ref, q_ref, ck_ref, cv_ref, nk_ref, nv_ref, qt_ref, m_ref, l_ref, acc_ref, turn_ref):
    for step in range(2):
        wide = q_ref[step].astype(jnp.float32)
        for g in range(GROUP):
            turn_ref[pl.ds(step * GROUP + g, ROWS, stride=2 * GROUP), :] = wide[:, 128 * g : 128 * g + 128]
    query = turn_ref[...].astype(jnp.bfloat16)
    qt_ref[...] = query
    dims = (((1,), (1,)), ((), ()))
    lanes = iota((16, 128), 1)
    parts = []
    for r in range(ROWS):
        score = lax.dot_general(
            query[16 * r : 16 * r + 16], ck_ref[r], dims, preferred_element_type=jnp.float32
        )
        parts.append(jnp.where(lanes < len_ref[r], score * SCORE_SCALE, MASKED_SCORE))
    score = jnp.concatenate(parts, axis=0)
    fresh_keys = jnp.concatenate([nk_ref[0], nk_ref[1]], axis=0)
    fresh_values = jnp.concatenate([nv_ref[0], nv_ref[1]], axis=0)
    fresh = lax.dot_general(query, fresh_keys, dims, preferred_element_type=jnp.float32) * SCORE_SCALE
    row, col = iota((QUERIES, 32), 0), iota((QUERIES, 32), 1)
    live = ((row >> 4) == (col & 15)) & ((col >> 4) <= ((row >> 3) & 1))
    fresh = jnp.where(live, fresh, MASKED_SCORE)
    peak = jnp.maximum(jnp.max(score, axis=1, keepdims=True), jnp.max(fresh, axis=1, keepdims=True))
    weight = jnp.exp2(score - peak)
    fresh_weight = jnp.exp2(fresh - peak)
    total = jnp.sum(weight, axis=1, keepdims=True) + jnp.sum(fresh_weight, axis=1, keepdims=True)
    m_ref[...] = jnp.broadcast_to(peak, (QUERIES, 128))
    l_ref[...] = jnp.broadcast_to(total, (QUERIES, 128))
    weight = weight.astype(jnp.bfloat16)
    acc = jnp.concatenate(
        [
            jnp.dot(weight[16 * r : 16 * r + 16], cv_ref[r], preferred_element_type=jnp.float32)
            for r in range(ROWS)
        ],
        axis=0,
    )
    acc_ref[...] = acc + jnp.dot(
        fresh_weight.astype(jnp.bfloat16), fresh_values, preferred_element_type=jnp.float32
    )


def resident(lengths, queries, cache_keys, cache_values, new_keys, new_values):
    wide = jax.ShapeDtypeStruct((QUERIES, 128), jnp.float32)
    return pl.pallas_call(
        resident_kernel,
        out_shape=(jax.ShapeDtypeStruct((QUERIES, 128), jnp.bfloat16), wide, wide, wide),
        in_specs=[SMEM] + [VMEM] * 5,
        out_specs=(VMEM,) * 4,
        scratch_shapes=[pltpu.VMEM((QUERIES, 128), jnp.float32)],
        compiler_params=PARAMS,
        cost_estimate=pl.CostEstimate(flops=20_000_000, bytes_accessed=1_500_000, transcendentals=40_000),
        name="resident",
    )(lengths, queries, cache_keys, cache_values, new_keys, new_values)


def merge_kernel(code_ref, recv_ref, q_ref, m_ref, l_ref, acc_ref, out_ref, turn_ref):
    wide = recv_ref[...].astype(jnp.float32).reshape(SLOTS, 2, 8, 128)
    even, odd = wide[:, 0], wide[:, 1]
    is_key = (iota((SLOTS, 8, 128), 1) & 1) == 0
    keys = jnp.where(is_key, even, pltpu.roll(odd, 1, 1)).reshape(SLOTS * 8, 128).astype(jnp.bfloat16)
    values = jnp.where(is_key, pltpu.roll(even, 7, 1), odd).reshape(SLOTS * 8, 128).astype(jnp.bfloat16)
    half = QUERIES // 2
    for request in range(2):
        rows = pl.ds(request * half, half)
        code = code_ref[...]
        length = jnp.where((code >> 4) == request, code & 15, 0)
        live = jnp.concatenate([length > t for t in range(8)], axis=1)
        score = lax.dot_general(
            q_ref[rows, :], keys, (((1,), (1,)), ((), ())), preferred_element_type=jnp.float32
        )
        score = jnp.where(live, score * SCORE_SCALE, MASKED_SCORE)
        old = m_ref[rows, :][:, 0:1]
        peak = jnp.maximum(jnp.max(score, axis=1, keepdims=True), old)
        weight = jnp.exp2(score - peak)
        keep = jnp.exp2(old - peak)
        total = jnp.sum(weight, axis=1, keepdims=True) + l_ref[rows, :][:, 0:1] * keep
        acc = jnp.dot(weight.astype(jnp.bfloat16), values, preferred_element_type=jnp.float32)
        turn_ref[rows, :] = (acc + acc_ref[rows, :] * keep) / total
    for step in range(2):
        for g in range(GROUP):
            out_ref[step, :, 128 * g : 128 * g + 128] = turn_ref[
                pl.ds(step * GROUP + g, ROWS, stride=2 * GROUP), :
            ].astype(jnp.bfloat16)


def merge(codes, received, query, peak, total, acc):
    return pl.pallas_call(
        merge_kernel,
        out_shape=jax.ShapeDtypeStruct((2, ROWS, GROUP * HEAD_DIM), jnp.bfloat16),
        in_specs=[VMEM] * 6,
        out_specs=VMEM,
        scratch_shapes=[pltpu.VMEM((QUERIES, 128), jnp.float32)],
        compiler_params=PARAMS,
        name="merge",
    )(codes, received, query, peak, total, acc)


def slot_codes(page_owner, page_request, page_length):
    own = lax.axis_index("pool")
    code = (page_length + 16 * page_request).reshape(POOL, PAGES)
    matched = page_owner.reshape(POOL, PAGES) == own
    position = iota((POOL, PAGES), 1)
    first = jnp.min(jnp.where(matched, position, PAGES), axis=1, keepdims=True)
    last = jnp.max(jnp.where(matched, position, -1), axis=1, keepdims=True)
    head = jnp.sum(jnp.where(position == first, code, 0), axis=1)
    tail = jnp.sum(jnp.where((position == last) & (last > first), code, 0), axis=1)
    slots = jnp.stack([head, tail], axis=1)
    return slots.reshape(16, 2, 2, 2).transpose(0, 2, 3, 1).reshape(1, SLOTS)


def body(
    queries,
    new_keys,
    new_values,
    cache_keys,
    cache_values,
    cache_lengths,
    handoff_kv,
    page_owner,
    page_request,
    page_length,
):
    pages = handoff_kv.reshape(PAGES, 2, KV_HEADS, 128).transpose(0, 2, 1, 3).reshape(PAGES * 16, 128)
    sent = pack(page_owner.reshape(24, 128), pages)
    arrived = lax.all_to_all(
        sent.reshape(TENSOR * POOL, 2 * CAP, 128), ("tensor", "pool"), split_axis=0, concat_axis=0, tiled=True
    )
    _, page_owner, page_request, page_length = lax.optimization_barrier(
        (sent, page_owner, page_request, page_length)
    )
    codes = slot_codes(page_owner, page_request, page_length)
    query, peak, total, acc = resident(cache_lengths, queries, cache_keys, cache_values, new_keys, new_values)
    return merge(codes, arrived.reshape(SLOTS * 16, 128), query, peak, total, acc)


def solution(mesh):
    return jax.shard_map(
        body,
        mesh=mesh,
        in_specs=(
            P(None, "pool", "tensor"),
            P(None, "pool", "tensor"),
            P(None, "pool", "tensor"),
            P("pool", None, "tensor"),
            P("pool", None, "tensor"),
            P("pool"),
            P("pool", None, "tensor", None, None),
            P(),
            P(),
            P(),
        ),
        out_specs=P(None, "pool", "tensor"),
        check_vma=False,
    )
```

time: 73.5 us -> 49.5 us (0.67)
  the two profiles are of different devices: /device:TPU:8 before, /device:TPU:1 now
where the time goes in v1:
time: 49.5 us; the launch traced here: 49.2 us
  starting transfers between devices  22.2 us (45%)
  waiting for transfers between devices  18.5 us (37%)
  Pallas kernels  4.38 us (9%)
  local copies, waits for them, and re-layouts  3.65 us (7%)
    all_to_all x1, starting transfers between devices, body(): lax.all_to_all(sent.reshape(TENSOR * POOL, 2 * CAP, 128), ('tensor', 'poo...  22.2 us
    all_to_all x1, waiting for transfers between devices, body(): lax.all_to_all(sent.reshape(TENSOR * POOL, 2 * CAP, 128), ('tensor', 'poo...  18.5 us
    unnamed x22, local copies, waits for them, and re-layouts  2.81 us
    pallas_call x1, Pallas kernels, merge(): pl.pallas_call(merge_kernel, out_shape=jax.ShapeDtypeStruct((2, ROWS, GRO...  1.72 us
    pallas_call x1, Pallas kernels, pack(): pl.pallas_call(pack_kernel, out_shape=jax.ShapeDtypeStruct((KV_HEADS * SL...  1.37 us
    pallas_call x1, Pallas kernels, resident(): pl.pallas_call(resident_kernel, out_shape=(jax.ShapeDtypeStruct((QUERIES,...  1.29 us
  transfers between devices with their start and end apart: 1, of which 1 were waited for; matrix products, arithmetic and copies ran while one was open for 2% of the time, Pallas kernels for 3%

profile of v1, /device:TPU:1, one launch (start us, length us, event | category | flops | bytes accessed | tf_op | source)
XLA Modules:
  0.0 49.2 jit_solution(7057744456894028149)
XLA Ops:
  0.0 0.0 copy-start.2
  0.0 0.9 %copy-done.2 = bf16[1,48,1,2,1024]{4,3,2,1,0:T(2,128)(2,1)S(1)} copy-done((bf16[1,48,1,2,1024]{4,3,2,1,0:T(2,128)(2,1)S(1)}, bf16[1,48,1,2,1024]{4,3,2,1,0:T(2,128)(2,1)}, u32[]{:S(2)}) %copy-start.2) | copy-done | bytes 196632
  0.9 0.0 copy-start.4
  0.9 0.7 %copy-done.4 = s32[3072]{0:T(1024)S(1)} copy-done((s32[3072]{0:T(1024)S(1)}, s32[3072]{0:T(1024)}, u32[]{:S(2)}) %copy-start.4) | copy-done | bytes 12312
  1.6 0.0 copy-start.9
  1.6 0.0 copy-start.10
  1.6 1.4 %pack.1 = bf16[2048,128]{1,0:T(8,128)(2,1)} custom-call(s32[24,128]{1,0:T(8,128)S(1)} %bitcast.12, bf16[768,128]{1,0:T(8,128)(2,1)S(1)} %bitcast.11), custom_call_target="tpu_custom_call" | custom-call | tf_op jit(solution)/shard_map/pack/pallas_call | solution.py:81
  3.0 0.0 copy-start
  3.0 0.0 copy-start.1
  3.0 22.2 %all-to-all-start = ((bf16[512,4,128]{2,1,0:T(4,128)(2,1)}), bf16[512,4,128]{2,1,0:T(4,128)(2,1)S(1)}, u32[]{:S(2)}, u32[]{:S(2)}) async-start(bf16[512,4,128]{2,1,0:T(4,128)(2,1)} %bitcast.5), calls=%async_computation | async-start | bytes 1048576 | tf_op jit(solution)/shard_map/all_to_all | solution.py:215
  25.2 0.0 copy-done.9
  25.2 0.0 copy-done.10
  25.2 0.0 copy-start.5
  25.2 0.1 reshape.40
  25.3 0.6 %copy-done.5 = s32[3072]{0:T(1024)S(1)} copy-done((s32[3072]{0:T(1024)S(1)}, s32[3072]{0:T(1024)}, u32[]{:S(2)}) %copy-start.5) | copy-done | bytes 12312
  25.9 0.1 eq.27
  26.0 0.1 select_reduce_fusion.3
  26.2 0.2 select_reduce_fusion.2
  26.4 0.1 stack.10
  26.5 0.0 copy-start.3
  26.5 0.1 copy.17
  26.6 0.1 stack.9
  26.7 0.1 copy.16
  26.8 0.1 copy.18
  26.9 0.0 copy-start.6
  26.9 0.0 copy-start.7
  27.0 0.0 copy-start.8
  27.0 0.1 reshape.41.code_ref
  27.1 0.0 copy-done
  27.1 0.0 copy-done.1
  27.1 0.2 copy-done.3
  27.3 0.3 copy-done.6
  27.6 0.0 copy-done.7
  27.7 0.0 copy-done.8
  27.7 1.3 %resident.1 = (bf16[256,128]{1,0:T(8,128)(2,1)S(1)}, f32[256,128]{1,0:T(8,128)S(1)}, f32[256,128]{1,0:T(8,128)S(1)}, f32[256,128]{1,0:T(8,128)S(1)}) custom-call(s32[16]{0:T(128)S(1)} %copy-done.8, bf16[2,16,1024]{2,1,0:T(8,128)(2,1)S(1)} %copy-done.3, bf16[16,128,128]{2,1,0:T(8,128)(2,1)S(1)} %copy-done, bf16[16,128,128]{2,1,0:T(8,128)(2,1)S(1)} %copy-done.1, ...), custom_call_target="tpu_custom_call" | custom-call | flops 20000000 | bytes 1500000 | tf_op jit(solution)/shard_map/resident/pallas_call | solution.py:134
  29.0 18.5 %all-to-all-done = bf16[512,4,128]{2,1,0:T(4,128)(2,1)S(1)} async-done(((bf16[512,4,128]{2,1,0:T(4,128)(2,1)}), bf16[512,4,128]{2,1,0:T(4,128)(2,1)S(1)}, u32[]{:S(2)}, u32[]{:S(2)}) %all-to-all-start) | async-done | bytes 524320 | tf_op jit(solution)/shard_map/all_to_all | solution.py:215
  47.5 1.7 %merge.1 = bf16[2,16,1024]{2,1,0:T(8,128)(2,1)} custom-call(s32[1,128]{1,0:T(1,128)S(1)} %reshape.41.code_ref, bf16[2048,128]{1,0:T(8,128)(2,1)S(1)} %bitcast.10, bf16[256,128]{1,0:T(8,128)(2,1)S(1)} %get-tuple-element.15.q_ref, f32[256,128]{1,0:T(8,128)S(1)} %get-tuple-element.16.m_ref, f32[256,128]{1,0:T(8,128)S(1)} %get-tuple-element.17.l_ref, ...), custom_call_target="tpu_custom_call" | custom-call | tf_op jit(solution)/shard_map/merge/pallas_call | solution.py:177
  (4 shorter events, 0.0 us)
Async XLA Ops:
  0.0 0.9 %copy-start.2 = (bf16[1,48,1,2,1024]{4,3,2,1,0:T(2,128)(2,1)S(1)}, bf16[1,48,1,2,1024]{4,3,2,1,0:T(2,128)(2,1)}, u32[]{:S(2)}) copy-start(bf16[1,48,1,2,1024]{4,3,2,1,0:T(2,128)(2,1)} %param.16) | copy-start | bytes 589828
  0.9 0.7 %copy-start.4 = (s32[3072]{0:T(1024)S(1)}, s32[3072]{0:T(1024)}, u32[]{:S(2)}) copy-start(s32[3072]{0:T(1024)} %param.17) | copy-start | bytes 36868
  1.6 23.6 %copy-start.9 = (s32[3072]{0:T(1024)S(1)}, s32[3072]{0:T(1024)}, u32[]{:S(2)}) copy-start(s32[3072]{0:T(1024)} %param.19) | copy-start | bytes 36868
  1.6 23.6 %copy-start.10 = (s32[3072]{0:T(1024)S(1)}, s32[3072]{0:T(1024)}, u32[]{:S(2)}) copy-start(s32[3072]{0:T(1024)} %param.18) | copy-start | bytes 36868
  3.0 24.1 %copy-start = (bf16[16,128,128]{2,1,0:T(8,128)(2,1)S(1)}, bf16[16,128,128]{2,1,0:T(8,128)(2,1)}, u32[]{:S(2)}) copy-start(bf16[16,128,128]{2,1,0:T(8,128)(2,1)} %ck_ref.1) | copy-start | bytes 1572868
  3.0 24.1 %copy-start.1 = (bf16[16,128,128]{2,1,0:T(8,128)(2,1)S(1)}, bf16[16,128,128]{2,1,0:T(8,128)(2,1)}, u32[]{:S(2)}) copy-start(bf16[16,128,128]{2,1,0:T(8,128)(2,1)} %cv_ref.1) | copy-start | bytes 1572868
  3.0 44.5 %all-to-all-start = ((bf16[512,4,128]{2,1,0:T(4,128)(2,1)}), bf16[512,4,128]{2,1,0:T(4,128)(2,1)S(1)}, u32[]{:S(2)}, u32[]{:S(2)}) async-start(bf16[512,4,128]{2,1,0:T(4,128)(2,1)} %bitcast.5), calls=%async_computation | async-start | bytes 1048576 | tf_op jit(solution)/shard_map/all_to_all | solution.py:215
  25.2 0.7 %copy-start.5 = (s32[3072]{0:T(1024)S(1)}, s32[3072]{0:T(1024)}, u32[]{:S(2)}) copy-start(s32[3072]{0:T(1024)} %param.17) | copy-start | bytes 36868
  26.5 0.8 %copy-start.3 = (bf16[2,16,1024]{2,1,0:T(8,128)(2,1)S(1)}, bf16[2,16,1024]{2,1,0:T(8,128)(2,1)}, u32[]{:S(2)}) copy-start(bf16[2,16,1024]{2,1,0:T(8,128)(2,1)} %q_ref.1) | copy-start | bytes 196612
  26.9 0.7 %copy-start.6 = (bf16[2,16,128]{2,1,0:T(8,128)(2,1)S(1)}, bf16[2,16,128]{2,1,0:T(8,128)(2,1)}, u32[]{:S(2)}) copy-start(bf16[2,16,128]{2,1,0:T(8,128)(2,1)} %nk_ref.1) | copy-start | bytes 24580
  26.9 0.7 %copy-start.7 = (bf16[2,16,128]{2,1,0:T(8,128)(2,1)S(1)}, bf16[2,16,128]{2,1,0:T(8,128)(2,1)}, u32[]{:S(2)}) copy-start(bf16[2,16,128]{2,1,0:T(8,128)(2,1)} %nv_ref.1) | copy-start | bytes 24580
  27.0 0.7 %copy-start.8 = (s32[16]{0:T(128)S(1)}, s32[16]{0:T(128)}, u32[]{:S(2)}) copy-start(s32[16]{0:T(128)} %len_ref.1) | copy-start | bytes 196

commit v2 on v1

--- a/solution.py
+++ b/solution.py
@@ -24,6 +24,7 @@
 
 VMEM = pl.BlockSpec(memory_space=pltpu.VMEM)
 SMEM = pl.BlockSpec(memory_space=pltpu.SMEM)
+HBM = pl.BlockSpec(memory_space=pltpu.HBM)
 PARAMS = pltpu.CompilerParams(vmem_limit_bytes=32 * 1024 * 1024)
 
 
@@ -31,10 +32,15 @@
     return lax.broadcasted_iota(jnp.int32, shape, axis)
 
 
-def pack_kernel(owner_ref, pages_ref, out_ref):
+def pack_kernel(owner_hbm, pages_hbm, out_hbm, owner_ref, pages_ref, wide_ref, out_ref, sems):
+    fetch_pages = pltpu.make_async_copy(pages_hbm, pages_ref, sems.at[0])
+    fetch_owners = pltpu.make_async_copy(owner_hbm, owner_ref, sems.at[1])
+    fetch_owners.start()
+    fetch_pages.start()
     start = lax.axis_index("pool") * PAGES
     row, lane = start // 128, lax.rem(start, 128)
     shift = lax.rem(128 - lane, 128)
+    fetch_owners.wait()
     first = jnp.broadcast_to(owner_ref[pl.ds(row, 1), :], (8, 128))
     second = jnp.broadcast_to(owner_ref[pl.ds(jnp.minimum(row + 1, 23), 1), :], (8, 128))
     lanes = iota((8, 128), 1)
@@ -49,22 +55,18 @@
         lanes < PAGES, key, jnp.where(lanes < 2 * PAGES, pltpu.roll(key, PAGES, 1) + 1, -1)
     )
     slots = jnp.where(iota((2 * SLOTS, 128), 0) == target[0:1], 1.0, 0.0).astype(jnp.bfloat16)
-    new = iota((256, 256), 0)
-    old = iota((256, 256), 1)
-    wanted = (new & 15) * 16 + (new >> 5) * 2 + ((new >> 4) & 1)
-    swap = jnp.where(old == wanted, 1.0, 0.0).astype(jnp.bfloat16)
-    turned = [
-        jnp.dot(swap, pages_ref[256 * i : 256 * (i + 1), :], preferred_element_type=jnp.float32).astype(
-            jnp.bfloat16
-        )
-        for i in range(3)
-    ]
+    fetch_pages.wait()
+    wide_ref[...] = pages_ref[...].astype(jnp.float32)
     zeros = jnp.zeros((128 - 2 * PAGES, 128), jnp.bfloat16)
+    stores = []
     for head in range(0, KV_HEADS, 2):
         block = jnp.concatenate(
             [
                 jnp.concatenate(
-                    [turned[i][32 * h + 16 * kv : 32 * h + 16 * kv + 16] for kv in range(2) for i in range(3)]
+                    [
+                        wide_ref[pl.ds(2 * h + kv, PAGES, stride=2 * KV_HEADS), :].astype(jnp.bfloat16)
+                        for kv in range(2)
+                    ]
                     + [zeros],
                     axis=0,
                 )
@@ -75,15 +77,26 @@
         placed = jnp.dot(slots, block, preferred_element_type=jnp.float32).astype(jnp.bfloat16)
         out_ref[head * 256 : head * 256 + 256, :] = placed[:, 0:128]
         out_ref[head * 256 + 256 : head * 256 + 512, :] = placed[:, 128:256]
+        rows = pl.ds(head * 256, 512)
+        stores.append(pltpu.make_async_copy(out_ref.at[rows], out_hbm.at[rows], sems.at[2 + head // 2]))
+        stores[-1].start()
+    for store in stores:
+        store.wait()
 
 
 def pack(owners, pages):
     return pl.pallas_call(
         pack_kernel,
         out_shape=jax.ShapeDtypeStruct((KV_HEADS * SLOTS * 2, 128), jnp.bfloat16),
-        in_specs=[VMEM, VMEM],
-        out_specs=VMEM,
-        compiler_params=PARAMS,
+        in_specs=[HBM, HBM],
+        out_specs=HBM,
+        scratch_shapes=[
+            pltpu.VMEM((24, 128), jnp.int32),
+            pltpu.VMEM((PAGES * 2 * KV_HEADS, 128), jnp.bfloat16),
+            pltpu.VMEM((PAGES * 2 * KV_HEADS, 128), jnp.float32),
+            pltpu.VMEM((KV_HEADS * SLOTS * 2, 128), jnp.bfloat16),
+            pltpu.SemaphoreType.DMA((6,)),
+        ],
         name="pack",
     )(owners, pages)
 
@@ -149,23 +162,23 @@
     is_key = (iota((SLOTS, 8, 128), 1) & 1) == 0
     keys = jnp.where(is_key, even, pltpu.roll(odd, 1, 1)).reshape(SLOTS * 8, 128).astype(jnp.bfloat16)
     values = jnp.where(is_key, pltpu.roll(even, 7, 1), odd).reshape(SLOTS * 8, 128).astype(jnp.bfloat16)
+    code = code_ref[...]
+    bias = []
+    for request in range(2):
+        length = jnp.where((code >> 4) == request, code & 15, 0)
+        bias.append(jnp.concatenate([jnp.where(length > t, 0.0, MASKED_SCORE) for t in range(8)], axis=1))
     half = QUERIES // 2
-    for request in range(2):
-        rows = pl.ds(request * half, half)
-        code = code_ref[...]
-        length = jnp.where((code >> 4) == request, code & 15, 0)
-        live = jnp.concatenate([length > t for t in range(8)], axis=1)
-        score = lax.dot_general(
-            q_ref[rows, :], keys, (((1,), (1,)), ((), ())), preferred_element_type=jnp.float32
-        )
-        score = jnp.where(live, score * SCORE_SCALE, MASKED_SCORE)
-        old = m_ref[rows, :][:, 0:1]
-        peak = jnp.maximum(jnp.max(score, axis=1, keepdims=True), old)
-        weight = jnp.exp2(score - peak)
-        keep = jnp.exp2(old - peak)
-        total = jnp.sum(weight, axis=1, keepdims=True) + l_ref[rows, :][:, 0:1] * keep
-        acc = jnp.dot(weight.astype(jnp.bfloat16), values, preferred_element_type=jnp.float32)
-        turn_ref[rows, :] = (acc + acc_ref[rows, :] * keep) / total
+    score = lax.dot_general(
+        q_ref[...], keys, (((1,), (1,)), ((), ())), preferred_element_type=jnp.float32
+    )
+    score = jnp.concatenate([score[:half] * SCORE_SCALE + bias[0], score[half:] * SCORE_SCALE + bias[1]], axis=0)
+    old = m_ref[...][:, 0:1]
+    peak = jnp.maximum(jnp.max(score, axis=1, keepdims=True), old)
+    weight = jnp.exp2(score - peak)
+    keep = jnp.exp2(old - peak)
+    total = jnp.sum(weight, axis=1, keepdims=True) + l_ref[...][:, 0:1] * keep
+    acc = jnp.dot(weight.astype(jnp.bfloat16), values, preferred_element_type=jnp.float32)
+    turn_ref[...] = (acc + acc_ref[...] * keep) / total
     for step in range(2):
         for g in range(GROUP):
             out_ref[step, :, 128 * g : 128 * g + 128] = turn_ref[

time: 49.5 us -> 48.4 us (0.978)
  local copies, waits for them, and re-layouts: 3.65 us -> 2.02 us
  Pallas kernels: 4.38 us -> 4.91 us
    unnamed x22 -> x18, local copies, waits for them, and re-layouts: 2.81 us -> 1.19 us
    pallas_call x1, Pallas kernels: 1.37 us -> 2.12 us  [pack(): pl.pallas_call(pack_kernel, out_shape=jax.ShapeDtypeStruct((KV_HEADS * SL...]
where the time goes in v2:
time: 48.4 us; the launch traced here: 48.2 us
  starting transfers between devices  22.2 us (46%)
  waiting for transfers between devices  18.6 us (38%)
  Pallas kernels  4.91 us (10%)
  local copies, waits for them, and re-layouts  2.02 us (4%)
    all_to_all x1, starting transfers between devices, body(): lax.all_to_all(sent.reshape(TENSOR * POOL, 2 * CAP, 128), ('tensor', 'poo...  22.2 us
    all_to_all x1, waiting for transfers between devices, body(): lax.all_to_all(sent.reshape(TENSOR * POOL, 2 * CAP, 128), ('tensor', 'poo...  18.6 us
    pallas_call x1, Pallas kernels, pack(): pl.pallas_call(pack_kernel, out_shape=jax.ShapeDtypeStruct((KV_HEADS * SL...  2.12 us
    pallas_call x1, Pallas kernels, merge(): pl.pallas_call(merge_kernel, out_shape=jax.ShapeDtypeStruct((2, ROWS, GRO...  1.5 us
    pallas_call x1, Pallas kernels, resident(): pl.pallas_call(resident_kernel, out_shape=(jax.ShapeDtypeStruct((QUERIES,...  1.29 us
    unnamed x18, local copies, waits for them, and re-layouts  1.19 us
  transfers between devices with their start and end apart: 1, of which 1 were waited for; matrix products, arithmetic and copies ran while one was open for 2% of the time, Pallas kernels for 3%

profile of v2, /device:TPU:1, one launch (start us, length us, event | category | flops | bytes accessed | tf_op | source)
XLA Modules:
  0.0 48.2 jit_solution(7999141032972544347)
XLA Ops:
  0.0 0.0 copy-start.7
  0.0 0.0 copy-start.8
  0.0 2.1 %pack.1 = bf16[2048,128]{1,0:T(8,128)(2,1)} custom-call(s32[24,128]{1,0:T(8,128)} %bitcast.13, bf16[768,128]{1,0:T(8,128)(2,1)} %bitcast.12), custom_call_target="tpu_custom_call" | custom-call | tf_op jit(solution)/shard_map/pack/pallas_call | solution.py:88
  2.1 0.0 copy-start
  2.1 0.0 copy-start.1
  2.2 22.2 %all-to-all-start = ((bf16[512,4,128]{2,1,0:T(4,128)(2,1)}), bf16[512,4,128]{2,1,0:T(4,128)(2,1)S(1)}, u32[]{:S(2)}, u32[]{:S(2)}) async-start(bf16[512,4,128]{2,1,0:T(4,128)(2,1)} %bitcast.11), calls=%async_computation | async-start | bytes 1048576 | tf_op jit(solution)/shard_map/all_to_all | solution.py:228
  24.3 0.0 copy-done.7
  24.3 0.0 copy-done.8
  24.4 0.0 copy-start.6
  24.4 0.1 reshape.40
  24.5 0.6 %copy-done.6 = s32[3072]{0:T(1024)S(1)} copy-done((s32[3072]{0:T(1024)S(1)}, s32[3072]{0:T(1024)}, u32[]{:S(2)}) %copy-start.6) | copy-done | bytes 12312
  25.1 0.1 eq.27
  25.2 0.1 select_reduce_fusion.3
  25.3 0.2 select_reduce_fusion.2
  25.5 0.1 stack.10
  25.6 0.0 copy-start.2
  25.6 0.1 copy.17
  25.7 0.1 stack.9
  25.9 0.1 copy.16
  26.0 0.1 copy.18
  26.1 0.0 copy-start.3
  26.1 0.0 copy-start.4
  26.1 0.0 copy-start.5
  26.1 0.1 reshape.41.code_ref
  26.3 0.0 copy-done
  26.3 0.0 copy-done.1
  26.3 0.2 copy-done.2
  26.5 0.3 copy-done.3
  26.8 0.0 copy-done.4
  26.8 0.0 copy-done.5
  26.8 1.3 %resident.1 = (bf16[256,128]{1,0:T(8,128)(2,1)S(1)}, f32[256,128]{1,0:T(8,128)S(1)}, f32[256,128]{1,0:T(8,128)S(1)}, f32[256,128]{1,0:T(8,128)S(1)}) custom-call(s32[16]{0:T(128)S(1)} %copy-done.5, bf16[2,16,1024]{2,1,0:T(8,128)(2,1)S(1)} %copy-done.2, bf16[16,128,128]{2,1,0:T(8,128)(2,1)S(1)} %copy-done, bf16[16,128,128]{2,1,0:T(8,128)(2,1)S(1)} %copy-done.1, ...), custom_call_target="tpu_custom_call" | custom-call | flops 20000000 | bytes 1500000 | tf_op jit(solution)/shard_map/resident/pallas_call | solution.py:147
  28.1 18.6 %all-to-all-done = bf16[512,4,128]{2,1,0:T(4,128)(2,1)S(1)} async-done(((bf16[512,4,128]{2,1,0:T(4,128)(2,1)}), bf16[512,4,128]{2,1,0:T(4,128)(2,1)S(1)}, u32[]{:S(2)}, u32[]{:S(2)}) %all-to-all-start) | async-done | bytes 524320 | tf_op jit(solution)/shard_map/all_to_all | solution.py:228
  46.7 1.5 %merge.1 = bf16[2,16,1024]{2,1,0:T(8,128)(2,1)} custom-call(s32[1,128]{1,0:T(1,128)S(1)} %reshape.41.code_ref, bf16[2048,128]{1,0:T(8,128)(2,1)S(1)} %bitcast.10, bf16[256,128]{1,0:T(8,128)(2,1)S(1)} %get-tuple-element.15.q_ref, f32[256,128]{1,0:T(8,128)S(1)} %get-tuple-element.16.m_ref, f32[256,128]{1,0:T(8,128)S(1)} %get-tuple-element.17.l_ref, ...), custom_call_target="tpu_custom_call" | custom-call | tf_op jit(solution)/shard_map/merge/pallas_call | solution.py:190
  (4 shorter events, 0.0 us)
Async XLA Ops:
  0.0 24.3 %copy-start.7 = (s32[3072]{0:T(1024)S(1)}, s32[3072]{0:T(1024)}, u32[]{:S(2)}) copy-start(s32[3072]{0:T(1024)} %param.19) | copy-start | bytes 36868
  0.0 24.3 %copy-start.8 = (s32[3072]{0:T(1024)S(1)}, s32[3072]{0:T(1024)}, u32[]{:S(2)}) copy-start(s32[3072]{0:T(1024)} %param.18) | copy-start | bytes 36868
  2.1 24.1 %copy-start = (bf16[16,128,128]{2,1,0:T(8,128)(2,1)S(1)}, bf16[16,128,128]{2,1,0:T(8,128)(2,1)}, u32[]{:S(2)}) copy-start(bf16[16,128,128]{2,1,0:T(8,128)(2,1)} %ck_ref.1) | copy-start | bytes 1572868
  2.1 24.1 %copy-start.1 = (bf16[16,128,128]{2,1,0:T(8,128)(2,1)S(1)}, bf16[16,128,128]{2,1,0:T(8,128)(2,1)}, u32[]{:S(2)}) copy-start(bf16[16,128,128]{2,1,0:T(8,128)(2,1)} %cv_ref.1) | copy-start | bytes 1572868
  2.2 44.5 %all-to-all-start = ((bf16[512,4,128]{2,1,0:T(4,128)(2,1)}), bf16[512,4,128]{2,1,0:T(4,128)(2,1)S(1)}, u32[]{:S(2)}, u32[]{:S(2)}) async-start(bf16[512,4,128]{2,1,0:T(4,128)(2,1)} %bitcast.11), calls=%async_computation | async-start | bytes 1048576 | tf_op jit(solution)/shard_map/all_to_all | solution.py:228
  24.4 0.7 %copy-start.6 = (s32[3072]{0:T(1024)S(1)}, s32[3072]{0:T(1024)}, u32[]{:S(2)}) copy-start(s32[3072]{0:T(1024)} %param.17) | copy-start | bytes 36868
  25.6 0.8 %copy-start.2 = (bf16[2,16,1024]{2,1,0:T(8,128)(2,1)S(1)}, bf16[2,16,1024]{2,1,0:T(8,128)(2,1)}, u32[]{:S(2)}) copy-start(bf16[2,16,1024]{2,1,0:T(8,128)(2,1)} %q_ref.1) | copy-start | bytes 196612
  26.1 0.7 %copy-start.3 = (bf16[2,16,128]{2,1,0:T(8,128)(2,1)S(1)}, bf16[2,16,128]{2,1,0:T(8,128)(2,1)}, u32[]{:S(2)}) copy-start(bf16[2,16,128]{2,1,0:T(8,128)(2,1)} %nk_ref.1) | copy-start | bytes 24580
  26.1 0.7 %copy-start.4 = (bf16[2,16,128]{2,1,0:T(8,128)(2,1)S(1)}, bf16[2,16,128]{2,1,0:T(8,128)(2,1)}, u32[]{:S(2)}) copy-start(bf16[2,16,128]{2,1,0:T(8,128)(2,1)} %nv_ref.1) | copy-start | bytes 24580
  26.1 0.7 %copy-start.5 = (s32[16]{0:T(128)S(1)}, s32[16]{0:T(128)}, u32[]{:S(2)}) copy-start(s32[16]{0:T(128)} %len_ref.1) | copy-start | bytes 196

commit v3 on v2

--- a/solution.py
+++ b/solution.py
@@ -21,6 +21,10 @@
 
 MASKED_SCORE = -1e30
 SCORE_SCALE = HEAD_DIM ** (-0.5) * 1.4426950408889634
+
+POOL_ORDER = [(y * 8 + z) * 2 + core for core in range(2) for z in range(8) for y in range(4)]
+HEAD_ORDER = [half * 4 + x for x in range(4) for half in range(2)]
+EXCHANGE = [[p * TENSOR + t for p in POOL_ORDER for t in HEAD_ORDER]]
 
 VMEM = pl.BlockSpec(memory_space=pltpu.VMEM)
 SMEM = pl.BlockSpec(memory_space=pltpu.SMEM)
@@ -49,7 +53,8 @@
     down = across.T
     earlier = iota((128, 128), 0) < iota((128, 128), 1)
     rank = jnp.sum(jnp.where((across == down) & earlier, 1.0, 0.0), axis=0, keepdims=True)
-    key = (owners * (2 * CAP)).astype(jnp.float32) + 2.0 * rank
+    place = (owners & 1) * 32 + ((owners >> 1) & 7) * 4 + (owners >> 4)
+    key = (place * (2 * CAP)).astype(jnp.float32) + 2.0 * rank
     key = key.astype(jnp.int32)
     target = jnp.where(
         lanes < PAGES, key, jnp.where(lanes < 2 * PAGES, pltpu.roll(key, PAGES, 1) + 1, -1)
@@ -58,27 +63,37 @@
     fetch_pages.wait()
     wide_ref[...] = pages_ref[...].astype(jnp.float32)
     zeros = jnp.zeros((128 - 2 * PAGES, 128), jnp.bfloat16)
+    first_half = iota((POOL // 2, 8, 128), 1) < 4
     stores = []
-    for head in range(0, KV_HEADS, 2):
-        block = jnp.concatenate(
-            [
-                jnp.concatenate(
-                    [
-                        wide_ref[pl.ds(2 * h + kv, PAGES, stride=2 * KV_HEADS), :].astype(jnp.bfloat16)
-                        for kv in range(2)
-                    ]
-                    + [zeros],
-                    axis=0,
-                )
-                for h in (head, head + 1)
-            ],
-            axis=1,
+    for part in range(2):
+        low, high = [], []
+        for pair in range(2):
+            heads = HEAD_ORDER[4 * part + 2 * pair : 4 * part + 2 * pair + 2]
+            block = jnp.concatenate(
+                [
+                    jnp.concatenate(
+                        [
+                            wide_ref[pl.ds(2 * h + kv, PAGES, stride=2 * KV_HEADS), :].astype(jnp.bfloat16)
+                            for kv in range(2)
+                        ]
+                        + [zeros],
+                        axis=0,
+                    )
+                    for h in heads
+                ],
+                axis=1,
+            )
+            placed = jnp.dot(slots, block, preferred_element_type=jnp.float32)
+            left = placed[:, 0:128].reshape(POOL // 2, 8, 128)
+            right = placed[:, 128:256].reshape(POOL // 2, 8, 128)
+            low.append(jnp.where(first_half, left, pltpu.roll(right, 4, 1)))
+            high.append(jnp.where(first_half, pltpu.roll(left, 4, 1), right))
+        rows = pl.ds(16 * part, 16)
+        out_ref[:, 0, rows, :] = jnp.concatenate(low, axis=1).astype(jnp.bfloat16)
+        out_ref[:, 1, rows, :] = jnp.concatenate(high, axis=1).astype(jnp.bfloat16)
+        stores.append(
+            pltpu.make_async_copy(out_ref.at[:, :, rows], out_hbm.at[:, :, rows], sems.at[2 + part])
         )
-        placed = jnp.dot(slots, block, preferred_element_type=jnp.float32).astype(jnp.bfloat16)
-        out_ref[head * 256 : head * 256 + 256, :] = placed[:, 0:128]
-        out_ref[head * 256 + 256 : head * 256 + 512, :] = placed[:, 128:256]
-        rows = pl.ds(head * 256, 512)
-        stores.append(pltpu.make_async_copy(out_ref.at[rows], out_hbm.at[rows], sems.at[2 + head // 2]))
         stores[-1].start()
     for store in stores:
         store.wait()
@@ -87,15 +102,15 @@
 def pack(owners, pages):
     return pl.pallas_call(
         pack_kernel,
-        out_shape=jax.ShapeDtypeStruct((KV_HEADS * SLOTS * 2, 128), jnp.bfloat16),
+        out_shape=jax.ShapeDtypeStruct((POOL // 2, 2, 4 * KV_HEADS, 128), jnp.bfloat16),
         in_specs=[HBM, HBM],
         out_specs=HBM,
         scratch_shapes=[
             pltpu.VMEM((24, 128), jnp.int32),
             pltpu.VMEM((PAGES * 2 * KV_HEADS, 128), jnp.bfloat16),
             pltpu.VMEM((PAGES * 2 * KV_HEADS, 128), jnp.float32),
-            pltpu.VMEM((KV_HEADS * SLOTS * 2, 128), jnp.bfloat16),
-            pltpu.SemaphoreType.DMA((6,)),
+            pltpu.VMEM((POOL // 2, 2, 4 * KV_HEADS, 128), jnp.bfloat16),
+            pltpu.SemaphoreType.DMA((4,)),
         ],
         name="pack",
     )(owners, pages)
@@ -106,8 +121,9 @@
         wide = q_ref[step].astype(jnp.float32)
         for g in range(GROUP):
             turn_ref[pl.ds(step * GROUP + g, ROWS, stride=2 * GROUP), :] = wide[:, 128 * g : 128 * g + 128]
+            block = pl.ds((step * GROUP + g) * ROWS, ROWS)
+            qt_ref[block, :] = q_ref[step, :, 128 * g : 128 * g + 128]
     query = turn_ref[...].astype(jnp.bfloat16)
-    qt_ref[...] = query
     dims = (((1,), (1,)), ((), ()))
     lanes = iota((16, 128), 1)
     parts = []
@@ -127,8 +143,6 @@
     weight = jnp.exp2(score - peak)
     fresh_weight = jnp.exp2(fresh - peak)
     total = jnp.sum(weight, axis=1, keepdims=True) + jnp.sum(fresh_weight, axis=1, keepdims=True)
-    m_ref[...] = jnp.broadcast_to(peak, (QUERIES, 128))
-    l_ref[...] = jnp.broadcast_to(total, (QUERIES, 128))
     weight = weight.astype(jnp.bfloat16)
     acc = jnp.concatenate(
         [
@@ -137,9 +151,11 @@
         ],
         axis=0,
     )
-    acc_ref[...] = acc + jnp.dot(
-        fresh_weight.astype(jnp.bfloat16), fresh_values, preferred_element_type=jnp.float32
-    )
+    acc = acc + jnp.dot(fresh_weight.astype(jnp.bfloat16), fresh_values, preferred_element_type=jnp.float32)
+    for result, result_ref in ((peak, m_ref), (total, l_ref), (acc, acc_ref)):
+        turn_ref[...] = jnp.broadcast_to(result, (QUERIES, 128))
+        for j in range(2 * GROUP):
+            result_ref[ROWS * j : ROWS * j + ROWS, :] = turn_ref[pl.ds(j, ROWS, stride=2 * GROUP), :]
 
 
 def resident(lengths, queries, cache_keys, cache_values, new_keys, new_values):
@@ -156,49 +172,42 @@
     )(lengths, queries, cache_keys, cache_values, new_keys, new_values)
 
 
-def merge_kernel(code_ref, recv_ref, q_ref, m_ref, l_ref, acc_ref, out_ref, turn_ref):
+def merge_kernel(bias_ref, recv_ref, q_ref, m_ref, l_ref, acc_ref, out_ref):
     wide = recv_ref[...].astype(jnp.float32).reshape(SLOTS, 2, 8, 128)
     even, odd = wide[:, 0], wide[:, 1]
     is_key = (iota((SLOTS, 8, 128), 1) & 1) == 0
     keys = jnp.where(is_key, even, pltpu.roll(odd, 1, 1)).reshape(SLOTS * 8, 128).astype(jnp.bfloat16)
     values = jnp.where(is_key, pltpu.roll(even, 7, 1), odd).reshape(SLOTS * 8, 128).astype(jnp.bfloat16)
-    code = code_ref[...]
-    bias = []
-    for request in range(2):
-        length = jnp.where((code >> 4) == request, code & 15, 0)
-        bias.append(jnp.concatenate([jnp.where(length > t, 0.0, MASKED_SCORE) for t in range(8)], axis=1))
-    half = QUERIES // 2
     score = lax.dot_general(
         q_ref[...], keys, (((1,), (1,)), ((), ())), preferred_element_type=jnp.float32
     )
-    score = jnp.concatenate([score[:half] * SCORE_SCALE + bias[0], score[half:] * SCORE_SCALE + bias[1]], axis=0)
+    bias = bias_ref[...].reshape(1, 2, 1, SLOTS * 8)
+    score = (score.reshape(2 * GROUP, 2, SAMPLES, SLOTS * 8) * SCORE_SCALE + bias).reshape(QUERIES, SLOTS * 8)
     old = m_ref[...][:, 0:1]
     peak = jnp.maximum(jnp.max(score, axis=1, keepdims=True), old)
     weight = jnp.exp2(score - peak)
     keep = jnp.exp2(old - peak)
     total = jnp.sum(weight, axis=1, keepdims=True) + l_ref[...][:, 0:1] * keep
     acc = jnp.dot(weight.astype(jnp.bfloat16), values, preferred_element_type=jnp.float32)
-    turn_ref[...] = (acc + acc_ref[...] * keep) / total
+    pieces = ((acc + acc_ref[...] * keep) / total).astype(jnp.bfloat16)
     for step in range(2):
         for g in range(GROUP):
-            out_ref[step, :, 128 * g : 128 * g + 128] = turn_ref[
-                pl.ds(step * GROUP + g, ROWS, stride=2 * GROUP), :
-            ].astype(jnp.bfloat16)
-
-
-def merge(codes, received, query, peak, total, acc):
+            at = (step * GROUP + g) * ROWS
+            out_ref[step, :, 128 * g : 128 * g + 128] = pieces[at : at + ROWS]
+
+
+def merge(bias, received, query, peak, total, acc):
     return pl.pallas_call(
         merge_kernel,
         out_shape=jax.ShapeDtypeStruct((2, ROWS, GROUP * HEAD_DIM), jnp.bfloat16),
         in_specs=[VMEM] * 6,
         out_specs=VMEM,
-        scratch_shapes=[pltpu.VMEM((QUERIES, 128), jnp.float32)],
         compiler_params=PARAMS,
         name="merge",
-    )(codes, received, query, peak, total, acc)
-
-
-def slot_codes(page_owner, page_request, page_length):
+    )(bias, received, query, peak, total, acc)
+
+
+def received_bias(page_owner, page_request, page_length):
     own = lax.axis_index("pool")
     code = (page_length + 16 * page_request).reshape(POOL, PAGES)
     matched = page_owner.reshape(POOL, PAGES) == own
@@ -207,8 +216,12 @@
     last = jnp.max(jnp.where(matched, position, -1), axis=1, keepdims=True)
     head = jnp.sum(jnp.where(position == first, code, 0), axis=1)
     tail = jnp.sum(jnp.where((position == last) & (last > first), code, 0), axis=1)
-    slots = jnp.stack([head, tail], axis=1)
-    return slots.reshape(16, 2, 2, 2).transpose(0, 2, 3, 1).reshape(1, SLOTS)
+    slots = jnp.stack([head, tail], axis=1).reshape(4, 8, 2, CAP).transpose(2, 1, 0, 3)
+    shape = (2, POOL, 2, 2, CAP, 2)
+    slots = jnp.broadcast_to(slots.reshape(1, POOL, 1, 1, CAP, 1), shape)
+    token = 4 * iota(shape, 3) + 2 * iota(shape, 2) + iota(shape, 5)
+    live = ((slots >> 4) == iota(shape, 0)) & ((slots & 15) > token)
+    return jnp.where(live, 0.0, MASKED_SCORE).reshape(2, SLOTS * 8)
 
 
 def body(
@@ -226,14 +239,19 @@
     pages = handoff_kv.reshape(PAGES, 2, KV_HEADS, 128).transpose(0, 2, 1, 3).reshape(PAGES * 16, 128)
     sent = pack(page_owner.reshape(24, 128), pages)
     arrived = lax.all_to_all(
-        sent.reshape(TENSOR * POOL, 2 * CAP, 128), ("tensor", "pool"), split_axis=0, concat_axis=0, tiled=True
+        sent.reshape(TENSOR * POOL, 2 * CAP, 128),
+        ("pool", "tensor"),
+        split_axis=0,
+        concat_axis=0,
+        axis_index_groups=EXCHANGE,
+        tiled=True,
     )
     _, page_owner, page_request, page_length = lax.optimization_barrier(
         (sent, page_owner, page_request, page_length)
     )
-    codes = slot_codes(page_owner, page_request, page_length)
+    bias = received_bias(page_owner, page_request, page_length)
     query, peak, total, acc = resident(cache_lengths, queries, cache_keys, cache_values, new_keys, new_values)
-    return merge(codes, arrived.reshape(SLOTS * 16, 128), query, peak, total, acc)
+    return merge(bias, arrived.reshape(SLOTS * 16, 128), query, peak, total, acc)
 
 
 def solution(mesh):

time: 48.4 us -> 47.7 us (0.986)
  waiting for transfers between devices: 18.6 us -> 17.1 us
    all_to_all x1, waiting for transfers between devices: 18.6 us -> 17.1 us  [body(): lax.all_to_all(sent.reshape(TENSOR * POOL, 2 * CAP, 128), ('pool', 'tenso...]
  transfers between devices with their start and end apart: 1 -> 1, of which waited for: 1 -> 1; matrix products, arithmetic and copies ran while one was open for 2% -> 4% of each run, Pallas kernels for 3% -> 3%
where the time goes in v3:
time: 47.7 us; the launch traced here: 47.4 us
  starting transfers between devices  22.2 us (47%)
  waiting for transfers between devices  17.1 us (36%)
  Pallas kernels  4.9 us (10%)
  local copies, waits for them, and re-layouts  2.43 us (5%)
  other arithmetic  0.59 us (1%)
    all_to_all x1, starting transfers between devices, body(): lax.all_to_all(sent.reshape(TENSOR * POOL, 2 * CAP, 128), ('pool', 'tenso...  22.2 us
    all_to_all x1, waiting for transfers between devices, body(): lax.all_to_all(sent.reshape(TENSOR * POOL, 2 * CAP, 128), ('pool', 'tenso...  17.1 us
    pallas_call x1, Pallas kernels, pack(): pl.pallas_call(pack_kernel, out_shape=jax.ShapeDtypeStruct((POOL // 2, 2,...  2.1 us
    pallas_call x1, Pallas kernels, merge(): pl.pallas_call(merge_kernel, out_shape=jax.ShapeDtypeStruct((2, ROWS, GRO...  1.48 us
    pallas_call x1, Pallas kernels, resident(): pl.pallas_call(resident_kernel, out_shape=(jax.ShapeDtypeStruct((QUERIES,...  1.32 us
    unnamed x18, local copies, waits for them, and re-layouts  0.97 us
  transfers between devices with their start and end apart: 1, of which 1 were waited for; matrix products, arithmetic and copies ran while one was open for 4% of the time, Pallas kernels for 3%

profile of v3, /device:TPU:1, one launch (start us, length us, event | category | flops | bytes accessed | tf_op | source)
XLA Modules:
  0.0 47.4 jit_solution(16200995226072191477)
XLA Ops:
  0.0 2.1 %pack.1 = bf16[32,2,32,128]{3,2,1,0:T(8,128)(2,1)} custom-call(s32[24,128]{1,0:T(8,128)} %bitcast.19, bf16[768,128]{1,0:T(8,128)(2,1)} %bitcast.16), custom_call_target="tpu_custom_call" | custom-call | tf_op jit(solution)/shard_map/pack/pallas_call | solution.py:103
  2.1 0.0 copy-start.7
  2.1 0.0 copy-start.8
  2.1 22.2 %all-to-all-start = ((bf16[512,4,128]{2,1,0:T(4,128)(2,1)}), bf16[512,4,128]{2,1,0:T(4,128)(2,1)S(1)}, u32[]{:S(2)}, u32[]{:S(2)}) async-start(bf16[512,4,128]{2,1,0:T(4,128)(2,1)} %bitcast.15), calls=%async_computation | async-start | bytes 1048576 | tf_op jit(solution)/shard_map/all_to_all | solution.py:241
  24.3 0.0 copy-done.7
  24.3 0.0 copy-done.8
  24.3 0.0 copy-start.6
  24.4 0.1 reshape.53
  24.4 0.6 %copy-done.6 = s32[3072]{0:T(1024)S(1)} copy-done((s32[3072]{0:T(1024)S(1)}, s32[3072]{0:T(1024)}, u32[]{:S(2)}) %copy-start.6) | copy-done | bytes 12312
  25.1 0.0 copy-start.2
  25.1 0.1 eq.31
  25.2 0.1 select_reduce_fusion.3
  25.3 0.0 copy-start.3
  25.3 0.0 copy-start.4
  25.3 0.2 select_reduce_fusion.2
  25.5 0.0 copy-start
  25.5 0.0 copy-start.1
  25.5 0.1 stack.10
  25.6 0.1 copy.23
  25.7 0.1 stack.9
  25.8 0.1 copy.22
  25.9 0.1 copy.29
  26.1 0.2 add_compare_fusion
  26.3 0.2 gt.18
  26.5 0.1 copy.28
  26.7 0.1 broadcast_in_dim.37
  26.8 0.0 copy-start.5
  26.8 0.3 broadcast_in_dim.38
  27.1 0.0 copy-done.2
  27.1 0.0 copy-done.3
  27.1 0.0 copy-done.4
  27.1 0.0 copy-done
  27.1 0.0 copy-done.1
  27.2 0.3 copy-done.5
  27.5 1.3 %resident.1 = (bf16[256,128]{1,0:T(8,128)(2,1)S(1)}, f32[256,128]{1,0:T(8,128)S(1)}, f32[256,128]{1,0:T(8,128)S(1)}, f32[256,128]{1,0:T(8,128)S(1)}) custom-call(s32[16]{0:T(128)S(1)} %copy-done.5, bf16[2,16,1024]{2,1,0:T(8,128)(2,1)S(1)} %copy-done.2, bf16[16,128,128]{2,1,0:T(8,128)(2,1)S(1)} %copy-done, bf16[16,128,128]{2,1,0:T(8,128)(2,1)S(1)} %copy-done.1, ...), custom_call_target="tpu_custom_call" | custom-call | flops 20000000 | bytes 1500000 | tf_op jit(solution)/shard_map/resident/pallas_call | solution.py:163
  28.8 17.1 %all-to-all-done = bf16[512,4,128]{2,1,0:T(4,128)(2,1)S(1)} async-done(((bf16[512,4,128]{2,1,0:T(4,128)(2,1)}), bf16[512,4,128]{2,1,0:T(4,128)(2,1)S(1)}, u32[]{:S(2)}, u32[]{:S(2)}) %all-to-all-start) | async-done | bytes 524320 | tf_op jit(solution)/shard_map/all_to_all | solution.py:241
  45.9 1.5 %merge.1 = bf16[2,16,1024]{2,1,0:T(8,128)(2,1)} custom-call(f32[2,1024]{1,0:T(2,128)S(1)} %and_select_fusion.bias_ref, bf16[2048,128]{1,0:T(8,128)(2,1)S(1)} %bitcast.14, bf16[256,128]{1,0:T(8,128)(2,1)S(1)} %get-tuple-element.15.q_ref, f32[256,128]{1,0:T(8,128)S(1)} %get-tuple-element.16.m_ref, f32[256,128]{1,0:T(8,128)S(1)} %get-tuple-element.17.l_ref, ...), custom_call_target="tpu_custom_call" | custom-call | tf_op jit(solution)/shard_map/merge/pallas_call | solution.py:200
  (6 shorter events, 0.0 us)
Async XLA Ops:
  2.1 22.2 %copy-start.7 = (s32[3072]{0:T(1024)S(1)}, s32[3072]{0:T(1024)}, u32[]{:S(2)}) copy-start(s32[3072]{0:T(1024)} %param.19) | copy-start | bytes 36868
  2.1 22.2 %copy-start.8 = (s32[3072]{0:T(1024)S(1)}, s32[3072]{0:T(1024)}, u32[]{:S(2)}) copy-start(s32[3072]{0:T(1024)} %param.18) | copy-start | bytes 36868
  2.1 43.8 %all-to-all-start = ((bf16[512,4,128]{2,1,0:T(4,128)(2,1)}), bf16[512,4,128]{2,1,0:T(4,128)(2,1)S(1)}, u32[]{:S(2)}, u32[]{:S(2)}) async-start(bf16[512,4,128]{2,1,0:T(4,128)(2,1)} %bitcast.15), calls=%async_computation | async-start | bytes 1048576 | tf_op jit(solution)/shard_map/all_to_all | solution.py:241
  24.3 0.7 %copy-start.6 = (s32[3072]{0:T(1024)S(1)}, s32[3072]{0:T(1024)}, u32[]{:S(2)}) copy-start(s32[3072]{0:T(1024)} %param.17) | copy-start | bytes 36868
  25.1 2.1 %copy-start.2 = (bf16[2,16,1024]{2,1,0:T(8,128)(2,1)S(1)}, bf16[2,16,1024]{2,1,0:T(8,128)(2,1)}, u32[]{:S(2)}) copy-start(bf16[2,16,1024]{2,1,0:T(8,128)(2,1)} %q_ref.1) | copy-start | bytes 196612
  25.3 1.8 %copy-start.3 = (bf16[2,16,128]{2,1,0:T(8,128)(2,1)S(1)}, bf16[2,16,128]{2,1,0:T(8,128)(2,1)}, u32[]{:S(2)}) copy-start(bf16[2,16,128]{2,1,0:T(8,128)(2,1)} %nk_ref.1) | copy-start | bytes 24580
  25.3 1.8 %copy-start.4 = (bf16[2,16,128]{2,1,0:T(8,128)(2,1)S(1)}, bf16[2,16,128]{2,1,0:T(8,128)(2,1)}, u32[]{:S(2)}) copy-start(bf16[2,16,128]{2,1,0:T(8,128)(2,1)} %nv_ref.1) | copy-start | bytes 24580
  25.5 1.6 %copy-start = (bf16[16,128,128]{2,1,0:T(8,128)(2,1)S(1)}, bf16[16,128,128]{2,1,0:T(8,128)(2,1)}, u32[]{:S(2)}) copy-start(bf16[16,128,128]{2,1,0:T(8,128)(2,1)} %ck_ref.1) | copy-start | bytes 1572868
  25.5 1.6 %copy-start.1 = (bf16[16,128,128]{2,1,0:T(8,128)(2,1)S(1)}, bf16[16,128,128]{2,1,0:T(8,128)(2,1)}, u32[]{:S(2)}) copy-start(bf16[16,128,128]{2,1,0:T(8,128)(2,1)} %cv_ref.1) | copy-start | bytes 1572868
  26.8 0.7 %copy-start.5 = (s32[16]{0:T(128)S(1)}, s32[16]{0:T(128)}, u32[]{:S(2)}) copy-start(s32[16]{0:T(128)} %len_ref.1) | copy-start | bytes 196

commit v4 on v3

--- a/solution.py
+++ b/solution.py
@@ -116,14 +116,13 @@
     )(owners, pages)
 
 
-def resident_kernel(len_ref, q_ref, ck_ref, cv_ref, nk_ref, nv_ref, qt_ref, m_ref, l_ref, acc_ref, turn_ref):
+def resident_kernel(len_ref, q_ref, ck_ref, nk_ref, nv_ref, qt_ref, score_ref, m_ref, fresh_ref, turn_ref):
     for step in range(2):
         wide = q_ref[step].astype(jnp.float32)
         for g in range(GROUP):
             turn_ref[pl.ds(step * GROUP + g, ROWS, stride=2 * GROUP), :] = wide[:, 128 * g : 128 * g + 128]
-            block = pl.ds((step * GROUP + g) * ROWS, ROWS)
-            qt_ref[block, :] = q_ref[step, :, 128 * g : 128 * g + 128]
     query = turn_ref[...].astype(jnp.bfloat16)
+    qt_ref[...] = query
     dims = (((1,), (1,)), ((), ()))
     lanes = iota((16, 128), 1)
     parts = []
@@ -133,46 +132,38 @@
         )
         parts.append(jnp.where(lanes < len_ref[r], score * SCORE_SCALE, MASKED_SCORE))
     score = jnp.concatenate(parts, axis=0)
-    fresh_keys = jnp.concatenate([nk_ref[0], nk_ref[1]], axis=0)
-    fresh_values = jnp.concatenate([nv_ref[0], nv_ref[1]], axis=0)
+    rest = jnp.zeros((128 - 2 * ROWS, 128), jnp.bfloat16)
+    fresh_keys = jnp.concatenate([nk_ref[0], nk_ref[1], rest], axis=0)
+    fresh_ref[...] = jnp.concatenate([nv_ref[0], nv_ref[1], rest], axis=0)
     fresh = lax.dot_general(query, fresh_keys, dims, preferred_element_type=jnp.float32) * SCORE_SCALE
-    row, col = iota((QUERIES, 32), 0), iota((QUERIES, 32), 1)
+    row, col = iota((QUERIES, 128), 0), iota((QUERIES, 128), 1)
     live = ((row >> 4) == (col & 15)) & ((col >> 4) <= ((row >> 3) & 1))
     fresh = jnp.where(live, fresh, MASKED_SCORE)
-    peak = jnp.maximum(jnp.max(score, axis=1, keepdims=True), jnp.max(fresh, axis=1, keepdims=True))
-    weight = jnp.exp2(score - peak)
-    fresh_weight = jnp.exp2(fresh - peak)
-    total = jnp.sum(weight, axis=1, keepdims=True) + jnp.sum(fresh_weight, axis=1, keepdims=True)
-    weight = weight.astype(jnp.bfloat16)
-    acc = jnp.concatenate(
-        [
-            jnp.dot(weight[16 * r : 16 * r + 16], cv_ref[r], preferred_element_type=jnp.float32)
-            for r in range(ROWS)
-        ],
-        axis=0,
-    )
-    acc = acc + jnp.dot(fresh_weight.astype(jnp.bfloat16), fresh_values, preferred_element_type=jnp.float32)
-    for result, result_ref in ((peak, m_ref), (total, l_ref), (acc, acc_ref)):
-        turn_ref[...] = jnp.broadcast_to(result, (QUERIES, 128))
-        for j in range(2 * GROUP):
-            result_ref[ROWS * j : ROWS * j + ROWS, :] = turn_ref[pl.ds(j, ROWS, stride=2 * GROUP), :]
-
-
-def resident(lengths, queries, cache_keys, cache_values, new_keys, new_values):
-    wide = jax.ShapeDtypeStruct((QUERIES, 128), jnp.float32)
+    score_ref[:, 0:128] = score
+    score_ref[:, 128:256] = fresh
+    peak = jnp.max(jnp.maximum(score, fresh), axis=1, keepdims=True)
+    m_ref[...] = jnp.broadcast_to(peak, (QUERIES, 128))
+
+
+def resident(lengths, queries, cache_keys, new_keys, new_values):
     return pl.pallas_call(
         resident_kernel,
-        out_shape=(jax.ShapeDtypeStruct((QUERIES, 128), jnp.bfloat16), wide, wide, wide),
-        in_specs=[SMEM] + [VMEM] * 5,
+        out_shape=(
+            jax.ShapeDtypeStruct((QUERIES, 128), jnp.bfloat16),
+            jax.ShapeDtypeStruct((QUERIES, 256), jnp.float32),
+            jax.ShapeDtypeStruct((QUERIES, 128), jnp.float32),
+            jax.ShapeDtypeStruct((128, 128), jnp.bfloat16),
+        ),
+        in_specs=[SMEM] + [VMEM] * 4,
         out_specs=(VMEM,) * 4,
         scratch_shapes=[pltpu.VMEM((QUERIES, 128), jnp.float32)],
         compiler_params=PARAMS,
-        cost_estimate=pl.CostEstimate(flops=20_000_000, bytes_accessed=1_500_000, transcendentals=40_000),
+        cost_estimate=pl.CostEstimate(flops=10_000_000, bytes_accessed=1_000_000, transcendentals=0),
         name="resident",
-    )(lengths, queries, cache_keys, cache_values, new_keys, new_values)
-
-
-def merge_kernel(bias_ref, recv_ref, q_ref, m_ref, l_ref, acc_ref, out_ref):
+    )(lengths, queries, cache_keys, new_keys, new_values)
+
+
+def merge_kernel(bias_ref, recv_ref, q_ref, score_ref, m_ref, cv_ref, fresh_ref, out_ref, turn_ref):
     wide = recv_ref[...].astype(jnp.float32).reshape(SLOTS, 2, 8, 128)
     even, odd = wide[:, 0], wide[:, 1]
     is_key = (iota((SLOTS, 8, 128), 1) & 1) == 0
@@ -181,30 +172,45 @@
     score = lax.dot_general(
         q_ref[...], keys, (((1,), (1,)), ((), ())), preferred_element_type=jnp.float32
     )
-    bias = bias_ref[...].reshape(1, 2, 1, SLOTS * 8)
-    score = (score.reshape(2 * GROUP, 2, SAMPLES, SLOTS * 8) * SCORE_SCALE + bias).reshape(QUERIES, SLOTS * 8)
-    old = m_ref[...][:, 0:1]
-    peak = jnp.maximum(jnp.max(score, axis=1, keepdims=True), old)
+    half = QUERIES // 2
+    score = jnp.concatenate(
+        [score[:half] * SCORE_SCALE + bias_ref[0:1, :], score[half:] * SCORE_SCALE + bias_ref[1:2, :]], axis=0
+    )
+    peak = jnp.maximum(jnp.max(score, axis=1, keepdims=True), m_ref[...][:, 0:1])
     weight = jnp.exp2(score - peak)
-    keep = jnp.exp2(old - peak)
-    total = jnp.sum(weight, axis=1, keepdims=True) + l_ref[...][:, 0:1] * keep
-    acc = jnp.dot(weight.astype(jnp.bfloat16), values, preferred_element_type=jnp.float32)
-    pieces = ((acc + acc_ref[...] * keep) / total).astype(jnp.bfloat16)
+    own = jnp.exp2(score_ref[...] - peak)
+    total = jnp.sum(weight, axis=1, keepdims=True) + jnp.sum(own, axis=1, keepdims=True)
+    own = own.astype(jnp.bfloat16)
+    held = jnp.concatenate(
+        [
+            jnp.dot(own[16 * r : 16 * r + 16, 0:128], cv_ref[r], preferred_element_type=jnp.float32)
+            for r in range(ROWS)
+        ],
+        axis=0,
+    )
+    acc = jnp.dot(
+        jnp.concatenate([weight.astype(jnp.bfloat16), own[:, 128:256]], axis=1),
+        jnp.concatenate([values, fresh_ref[...]], axis=0),
+        preferred_element_type=jnp.float32,
+    )
+    turn_ref[...] = (acc + held) / total
     for step in range(2):
         for g in range(GROUP):
-            at = (step * GROUP + g) * ROWS
-            out_ref[step, :, 128 * g : 128 * g + 128] = pieces[at : at + ROWS]
-
-
-def merge(bias, received, query, peak, total, acc):
+            out_ref[step, :, 128 * g : 128 * g + 128] = turn_ref[
+                pl.ds(step * GROUP + g, ROWS, stride=2 * GROUP), :
+            ].astype(jnp.bfloat16)
+
+
+def merge(bias, received, query, score, peak, cache_values, fresh_values):
     return pl.pallas_call(
         merge_kernel,
         out_shape=jax.ShapeDtypeStruct((2, ROWS, GROUP * HEAD_DIM), jnp.bfloat16),
-        in_specs=[VMEM] * 6,
+        in_specs=[VMEM] * 7,
         out_specs=VMEM,
+        scratch_shapes=[pltpu.VMEM((QUERIES, 128), jnp.float32)],
         compiler_params=PARAMS,
         name="merge",
-    )(bias, received, query, peak, total, acc)
+    )(bias, received, query, score, peak, cache_values, fresh_values)
 
 
 def received_bias(page_owner, page_request, page_length):
@@ -250,8 +256,8 @@
         (sent, page_owner, page_request, page_length)
     )
     bias = received_bias(page_owner, page_request, page_length)
-    query, peak, total, acc = resident(cache_lengths, queries, cache_keys, cache_values, new_keys, new_values)
-    return merge(bias, arrived.reshape(SLOTS * 16, 128), query, peak, total, acc)
+    query, score, peak, fresh_values = resident(cache_lengths, queries, cache_keys, new_keys, new_values)
+    return merge(bias, arrived.reshape(SLOTS * 16, 128), query, score, peak, cache_values, fresh_values)
 
 
 def solution(mesh):

time: 47.7 us -> 47.8 us (level)
  transfers between devices with their start and end apart: 1 -> 1, of which waited for: 1 -> 1; matrix products, arithmetic and copies ran while one was open for 4% -> 4% of each run, Pallas kernels for 3% -> 2%
where the time goes in v4:
time: 47.8 us; the launch traced here: 47.5 us
  starting transfers between devices  22.2 us (46%)
  waiting for transfers between devices  17.5 us (37%)
  Pallas kernels  4.73 us (10%)
  local copies, waits for them, and re-layouts  2.34 us (5%)
  other arithmetic  0.59 us (1%)
    all_to_all x1, starting transfers between devices, body(): lax.all_to_all(sent.reshape(TENSOR * POOL, 2 * CAP, 128), ('pool', 'tenso...  22.2 us
    all_to_all x1, waiting for transfers between devices, body(): lax.all_to_all(sent.reshape(TENSOR * POOL, 2 * CAP, 128), ('pool', 'tenso...  17.5 us
    pallas_call x1, Pallas kernels, pack(): pl.pallas_call(pack_kernel, out_shape=jax.ShapeDtypeStruct((POOL // 2, 2,...  2.1 us
    pallas_call x1, Pallas kernels, merge(): pl.pallas_call(merge_kernel, out_shape=jax.ShapeDtypeStruct((2, ROWS, GRO...  1.58 us
    pallas_call x1, Pallas kernels, resident(): pl.pallas_call(resident_kernel, out_shape=(jax.ShapeDtypeStruct((QUERIES,...  1.05 us
  transfers between devices with their start and end apart: 1, of which 1 were waited for; matrix products, arithmetic and copies ran while one was open for 4% of the time, Pallas kernels for 2%

profile of v4, /device:TPU:1, one launch (start us, length us, event | category | flops | bytes accessed | tf_op | source)
XLA Modules:
  0.0 47.5 jit_solution(5322294531390344877)
XLA Ops:
  0.0 2.1 %pack.1 = bf16[32,2,32,128]{3,2,1,0:T(8,128)(2,1)} custom-call(s32[24,128]{1,0:T(8,128)} %bitcast.19, bf16[768,128]{1,0:T(8,128)(2,1)} %bitcast.16), custom_call_target="tpu_custom_call" | custom-call | tf_op jit(solution)/shard_map/pack/pallas_call | solution.py:103
  2.1 0.0 copy-start.7
  2.1 0.0 copy-start.8
  2.1 22.2 %all-to-all-start = ((bf16[512,4,128]{2,1,0:T(4,128)(2,1)}), bf16[512,4,128]{2,1,0:T(4,128)(2,1)S(1)}, u32[]{:S(2)}, u32[]{:S(2)}) async-start(bf16[512,4,128]{2,1,0:T(4,128)(2,1)} %bitcast.15), calls=%async_computation | async-start | bytes 1048576 | tf_op jit(solution)/shard_map/all_to_all | solution.py:247
  24.3 0.0 copy-done.7
  24.3 0.0 copy-done.8
  24.3 0.0 copy-start.6
  24.4 0.1 reshape.53
  24.4 0.6 %copy-done.6 = s32[3072]{0:T(1024)S(1)} copy-done((s32[3072]{0:T(1024)S(1)}, s32[3072]{0:T(1024)}, u32[]{:S(2)}) %copy-start.6) | copy-done | bytes 12312
  25.1 0.1 eq.31
  25.2 0.1 select_reduce_fusion.3
  25.3 0.2 select_reduce_fusion.2
  25.5 0.0 copy-start.1
  25.5 0.1 stack.10
  25.6 0.1 copy.23
  25.7 0.1 stack.9
  25.8 0.1 copy.22
  25.9 0.1 copy.29
  26.0 0.2 add_compare_fusion
  26.3 0.2 gt.18
  26.5 0.0 copy-start.2
  26.5 0.0 copy-start.3
  26.5 0.0 copy-start.4
  26.5 0.0 copy-start.5
  26.5 0.1 copy.28
  26.7 0.0 copy-start
  26.7 0.1 broadcast_in_dim.37
  26.8 0.3 broadcast_in_dim.38
  27.1 0.0 copy-done.1
  27.1 0.2 copy-done.2
  27.3 0.0 copy-done.3
  27.3 0.0 copy-done.4
  27.3 0.0 copy-done.5
  27.3 1.1 %resident.1 = (bf16[256,128]{1,0:T(8,128)(2,1)S(1)}, f32[256,256]{1,0:T(8,128)S(1)}, f32[256,128]{1,0:T(8,128)S(1)}, bf16[128,128]{1,0:T(8,128)(2,1)S(1)}) custom-call(s32[16]{0:T(128)S(1)} %copy-done.5, bf16[2,16,1024]{2,1,0:T(8,128)(2,1)S(1)} %copy-done.2, bf16[16,128,128]{2,1,0:T(8,128)(2,1)S(1)} %copy-done.1, bf16[2,16,128]{2,1,0:T(8,128)(2,1)S(1)} %copy-done.3, ...), custom_call_target="tpu_custom_call" | custom-call | flops 10000000 | bytes 1000000 | tf_op jit(solution)/shard_map/resident/pallas_call | solution.py:149
  28.4 17.5 %all-to-all-done = bf16[512,4,128]{2,1,0:T(4,128)(2,1)S(1)} async-done(((bf16[512,4,128]{2,1,0:T(4,128)(2,1)}), bf16[512,4,128]{2,1,0:T(4,128)(2,1)S(1)}, u32[]{:S(2)}, u32[]{:S(2)}) %all-to-all-start) | async-done | bytes 524320 | tf_op jit(solution)/shard_map/all_to_all | solution.py:247
  45.9 0.0 copy-done
  45.9 1.6 %merge.1 = bf16[2,16,1024]{2,1,0:T(8,128)(2,1)} custom-call(f32[2,1024]{1,0:T(2,128)S(1)} %and_select_fusion.bias_ref, bf16[2048,128]{1,0:T(8,128)(2,1)S(1)} %bitcast.14, bf16[256,128]{1,0:T(8,128)(2,1)S(1)} %get-tuple-element.15.q_ref, f32[256,256]{1,0:T(8,128)S(1)} %get-tuple-element.16.score_ref, f32[256,128]{1,0:T(8,128)S(1)} %get-tuple-element.17.m_ref, ...), custom_call_target="tpu_custom_call" | custom-call | tf_op jit(solution)/shard_map/merge/pallas_call | solution.py:205
  (6 shorter events, 0.0 us)
Async XLA Ops:
  2.1 22.2 %copy-start.7 = (s32[3072]{0:T(1024)S(1)}, s32[3072]{0:T(1024)}, u32[]{:S(2)}) copy-start(s32[3072]{0:T(1024)} %param.19) | copy-start | bytes 36868
  2.1 22.2 %copy-start.8 = (s32[3072]{0:T(1024)S(1)}, s32[3072]{0:T(1024)}, u32[]{:S(2)}) copy-start(s32[3072]{0:T(1024)} %param.18) | copy-start | bytes 36868
  2.1 43.8 %all-to-all-start = ((bf16[512,4,128]{2,1,0:T(4,128)(2,1)}), bf16[512,4,128]{2,1,0:T(4,128)(2,1)S(1)}, u32[]{:S(2)}, u32[]{:S(2)}) async-start(bf16[512,4,128]{2,1,0:T(4,128)(2,1)} %bitcast.15), calls=%async_computation | async-start | bytes 1048576 | tf_op jit(solution)/shard_map/all_to_all | solution.py:247
  24.3 0.7 %copy-start.6 = (s32[3072]{0:T(1024)S(1)}, s32[3072]{0:T(1024)}, u32[]{:S(2)}) copy-start(s32[3072]{0:T(1024)} %param.17) | copy-start | bytes 36868
  25.5 1.6 %copy-start.1 = (bf16[16,128,128]{2,1,0:T(8,128)(2,1)S(1)}, bf16[16,128,128]{2,1,0:T(8,128)(2,1)}, u32[]{:S(2)}) copy-start(bf16[16,128,128]{2,1,0:T(8,128)(2,1)} %ck_ref.1) | copy-start | bytes 1572868
  26.5 0.8 %copy-start.2 = (bf16[2,16,1024]{2,1,0:T(8,128)(2,1)S(1)}, bf16[2,16,1024]{2,1,0:T(8,128)(2,1)}, u32[]{:S(2)}) copy-start(bf16[2,16,1024]{2,1,0:T(8,128)(2,1)} %q_ref.1) | copy-start | bytes 196612
  26.5 0.8 %copy-start.3 = (bf16[2,16,128]{2,1,0:T(8,128)(2,1)S(1)}, bf16[2,16,128]{2,1,0:T(8,128)(2,1)}, u32[]{:S(2)}) copy-start(bf16[2,16,128]{2,1,0:T(8,128)(2,1)} %nk_ref.1) | copy-start | bytes 24580
  26.5 0.8 %copy-start.4 = (bf16[2,16,128]{2,1,0:T(8,128)(2,1)S(1)}, bf16[2,16,128]{2,1,0:T(8,128)(2,1)}, u32[]{:S(2)}) copy-start(bf16[2,16,128]{2,1,0:T(8,128)(2,1)} %nv_ref.1) | copy-start | bytes 24580
  26.5 0.8 %copy-start.5 = (s32[16]{0:T(128)S(1)}, s32[16]{0:T(128)}, u32[]{:S(2)}) copy-start(s32[16]{0:T(128)} %len_ref.1) | copy-start | bytes 196
  26.7 19.3 %copy-start = (bf16[16,128,128]{2,1,0:T(8,128)(2,1)S(1)}, bf16[16,128,128]{2,1,0:T(8,128)(2,1)}, u32[]{:S(2)}) copy-start(bf16[16,128,128]{2,1,0:T(8,128)(2,1)} %cv_ref.1) | copy-start | bytes 1572868

commit v5 on v4

--- a/solution.py
+++ b/solution.py
@@ -1,3 +1,5 @@
+import functools
+
 import jax
 import jax.numpy as jnp
 from jax import lax
@@ -176,20 +178,23 @@
     score = jnp.concatenate(
         [score[:half] * SCORE_SCALE + bias_ref[0:1, :], score[half:] * SCORE_SCALE + bias_ref[1:2, :]], axis=0
     )
-    peak = jnp.maximum(jnp.max(score, axis=1, keepdims=True), m_ref[...][:, 0:1])
-    weight = jnp.exp2(score - peak)
-    own = jnp.exp2(score_ref[...] - peak)
-    total = jnp.sum(weight, axis=1, keepdims=True) + jnp.sum(own, axis=1, keepdims=True)
-    own = own.astype(jnp.bfloat16)
-    held = jnp.concatenate(
-        [
-            jnp.dot(own[16 * r : 16 * r + 16, 0:128], cv_ref[r], preferred_element_type=jnp.float32)
-            for r in range(ROWS)
-        ],
-        axis=0,
-    )
+    tiles = [score[:, 128 * t : 128 * t + 128] for t in range(8)]
+    peak = functools.reduce(jnp.maximum, tiles, m_ref[...])
+    peak = jnp.max(peak, axis=1, keepdims=True)
+    tiles = [jnp.exp2(tile - peak) for tile in tiles + [score_ref[:, 0:128], score_ref[:, 128:256]]]
+    total = jnp.sum(functools.reduce(jnp.add, tiles), axis=1, keepdims=True)
+    tiles = [tile.astype(jnp.bfloat16) for tile in tiles]
+    held = []
+    for r in range(0, ROWS, 2):
+        both = jnp.dot(
+            tiles[8][16 * r : 16 * r + 32],
+            jnp.concatenate([cv_ref[r], cv_ref[r + 1]], axis=1),
+            preferred_element_type=jnp.float32,
+        )
+        held += [both[0:16, 0:128], both[16:32, 128:256]]
+    held = jnp.concatenate(held, axis=0)
     acc = jnp.dot(
-        jnp.concatenate([weight.astype(jnp.bfloat16), own[:, 128:256]], axis=1),
+        jnp.concatenate(tiles[:8] + tiles[9:], axis=1),
         jnp.concatenate([values, fresh_ref[...]], axis=0),
         preferred_element_type=jnp.float32,
     )

time: 47.8 us -> 47.7 us (level)
  no operation moved by 1% of the time
where the time goes in v5:
time: 47.7 us; the launch traced here: 47.4 us
  starting transfers between devices  22.2 us (47%)
  waiting for transfers between devices  17.5 us (37%)
  Pallas kernels  4.63 us (10%)
  local copies, waits for them, and re-layouts  2.34 us (5%)
  other arithmetic  0.59 us (1%)
    all_to_all x1, starting transfers between devices, body(): lax.all_to_all(sent.reshape(TENSOR * POOL, 2 * CAP, 128), ('pool', 'tenso...  22.2 us
    all_to_all x1, waiting for transfers between devices, body(): lax.all_to_all(sent.reshape(TENSOR * POOL, 2 * CAP, 128), ('pool', 'tenso...  17.5 us
    pallas_call x1, Pallas kernels, pack(): pl.pallas_call(pack_kernel, out_shape=jax.ShapeDtypeStruct((POOL // 2, 2,...  2.1 us
    pallas_call x1, Pallas kernels, merge(): pl.pallas_call(merge_kernel, out_shape=jax.ShapeDtypeStruct((2, ROWS, GRO...  1.48 us
    pallas_call x1, Pallas kernels, resident(): pl.pallas_call(resident_kernel, out_shape=(jax.ShapeDtypeStruct((QUERIES,...  1.05 us
  transfers between devices with their start and end apart: 1, of which 1 were waited for; matrix products, arithmetic and copies ran while one was open for 4% of the time, Pallas kernels for 2%

profile of v5, /device:TPU:1, one launch (start us, length us, event | category | flops | bytes accessed | tf_op | source)
XLA Modules:
  0.0 47.4 jit_solution(17687347142747692206)
XLA Ops:
  0.0 2.1 %pack.1 = bf16[32,2,32,128]{3,2,1,0:T(8,128)(2,1)} custom-call(s32[24,128]{1,0:T(8,128)} %bitcast.19, bf16[768,128]{1,0:T(8,128)(2,1)} %bitcast.16), custom_call_target="tpu_custom_call" | custom-call | tf_op jit(solution)/shard_map/pack/pallas_call | solution.py:105
  2.1 0.0 copy-start.7
  2.1 0.0 copy-start.8
  2.1 22.2 %all-to-all-start = ((bf16[512,4,128]{2,1,0:T(4,128)(2,1)}), bf16[512,4,128]{2,1,0:T(4,128)(2,1)S(1)}, u32[]{:S(2)}, u32[]{:S(2)}) async-start(bf16[512,4,128]{2,1,0:T(4,128)(2,1)} %bitcast.15), calls=%async_computation | async-start | bytes 1048576 | tf_op jit(solution)/shard_map/all_to_all | solution.py:252
  24.3 0.0 copy-done.7
  24.3 0.0 copy-done.8
  24.3 0.0 copy-start.6
  24.4 0.1 reshape.53
  24.4 0.6 %copy-done.6 = s32[3072]{0:T(1024)S(1)} copy-done((s32[3072]{0:T(1024)S(1)}, s32[3072]{0:T(1024)}, u32[]{:S(2)}) %copy-start.6) | copy-done | bytes 12312
  25.1 0.1 eq.31
  25.2 0.1 select_reduce_fusion.3
  25.3 0.2 select_reduce_fusion.2
  25.5 0.0 copy-start.1
  25.5 0.1 stack.10
  25.6 0.1 copy.23
  25.7 0.1 stack.9
  25.8 0.1 copy.22
  25.9 0.1 copy.29
  26.0 0.2 add_compare_fusion
  26.3 0.2 gt.18
  26.5 0.0 copy-start.2
  26.5 0.0 copy-start.3
  26.5 0.0 copy-start.4
  26.5 0.0 copy-start.5
  26.5 0.1 copy.28
  26.7 0.0 copy-start
  26.7 0.1 broadcast_in_dim.37
  26.8 0.3 broadcast_in_dim.38
  27.1 0.0 copy-done.1
  27.1 0.2 copy-done.2
  27.3 0.0 copy-done.3
  27.3 0.0 copy-done.4
  27.3 0.0 copy-done.5
  27.3 1.1 %resident.1 = (bf16[256,128]{1,0:T(8,128)(2,1)S(1)}, f32[256,256]{1,0:T(8,128)S(1)}, f32[256,128]{1,0:T(8,128)S(1)}, bf16[128,128]{1,0:T(8,128)(2,1)S(1)}) custom-call(s32[16]{0:T(128)S(1)} %copy-done.5, bf16[2,16,1024]{2,1,0:T(8,128)(2,1)S(1)} %copy-done.2, bf16[16,128,128]{2,1,0:T(8,128)(2,1)S(1)} %copy-done.1, bf16[2,16,128]{2,1,0:T(8,128)(2,1)S(1)} %copy-done.3, ...), custom_call_target="tpu_custom_call" | custom-call | flops 10000000 | bytes 1000000 | tf_op jit(solution)/shard_map/resident/pallas_call | solution.py:151
  28.4 17.5 %all-to-all-done = bf16[512,4,128]{2,1,0:T(4,128)(2,1)S(1)} async-done(((bf16[512,4,128]{2,1,0:T(4,128)(2,1)}), bf16[512,4,128]{2,1,0:T(4,128)(2,1)S(1)}, u32[]{:S(2)}, u32[]{:S(2)}) %all-to-all-start) | async-done | bytes 524320 | tf_op jit(solution)/shard_map/all_to_all | solution.py:252
  45.9 0.0 copy-done
  45.9 1.5 %merge.1 = bf16[2,16,1024]{2,1,0:T(8,128)(2,1)} custom-call(f32[2,1024]{1,0:T(2,128)S(1)} %and_select_fusion.bias_ref, bf16[2048,128]{1,0:T(8,128)(2,1)S(1)} %bitcast.14, bf16[256,128]{1,0:T(8,128)(2,1)S(1)} %get-tuple-element.15.q_ref, f32[256,256]{1,0:T(8,128)S(1)} %get-tuple-element.16.score_ref, f32[256,128]{1,0:T(8,128)S(1)} %get-tuple-element.17.m_ref, ...), custom_call_target="tpu_custom_call" | custom-call | tf_op jit(solution)/shard_map/merge/pallas_call | solution.py:210
  (6 shorter events, 0.0 us)
Async XLA Ops:
  2.1 22.2 %copy-start.7 = (s32[3072]{0:T(1024)S(1)}, s32[3072]{0:T(1024)}, u32[]{:S(2)}) copy-start(s32[3072]{0:T(1024)} %param.19) | copy-start | bytes 36868
  2.1 22.2 %copy-start.8 = (s32[3072]{0:T(1024)S(1)}, s32[3072]{0:T(1024)}, u32[]{:S(2)}) copy-start(s32[3072]{0:T(1024)} %param.18) | copy-start | bytes 36868
  2.1 43.8 %all-to-all-start = ((bf16[512,4,128]{2,1,0:T(4,128)(2,1)}), bf16[512,4,128]{2,1,0:T(4,128)(2,1)S(1)}, u32[]{:S(2)}, u32[]{:S(2)}) async-start(bf16[512,4,128]{2,1,0:T(4,128)(2,1)} %bitcast.15), calls=%async_computation | async-start | bytes 1048576 | tf_op jit(solution)/shard_map/all_to_all | solution.py:252
  24.3 0.7 %copy-start.6 = (s32[3072]{0:T(1024)S(1)}, s32[3072]{0:T(1024)}, u32[]{:S(2)}) copy-start(s32[3072]{0:T(1024)} %param.17) | copy-start | bytes 36868
  25.5 1.6 %copy-start.1 = (bf16[16,128,128]{2,1,0:T(8,128)(2,1)S(1)}, bf16[16,128,128]{2,1,0:T(8,128)(2,1)}, u32[]{:S(2)}) copy-start(bf16[16,128,128]{2,1,0:T(8,128)(2,1)} %ck_ref.1) | copy-start | bytes 1572868
  26.5 0.8 %copy-start.2 = (bf16[2,16,1024]{2,1,0:T(8,128)(2,1)S(1)}, bf16[2,16,1024]{2,1,0:T(8,128)(2,1)}, u32[]{:S(2)}) copy-start(bf16[2,16,1024]{2,1,0:T(8,128)(2,1)} %q_ref.1) | copy-start | bytes 196612
  26.5 0.8 %copy-start.3 = (bf16[2,16,128]{2,1,0:T(8,128)(2,1)S(1)}, bf16[2,16,128]{2,1,0:T(8,128)(2,1)}, u32[]{:S(2)}) copy-start(bf16[2,16,128]{2,1,0:T(8,128)(2,1)} %nk_ref.1) | copy-start | bytes 24580
  26.5 0.8 %copy-start.4 = (bf16[2,16,128]{2,1,0:T(8,128)(2,1)S(1)}, bf16[2,16,128]{2,1,0:T(8,128)(2,1)}, u32[]{:S(2)}) copy-start(bf16[2,16,128]{2,1,0:T(8,128)(2,1)} %nv_ref.1) | copy-start | bytes 24580
  26.5 0.8 %copy-start.5 = (s32[16]{0:T(128)S(1)}, s32[16]{0:T(128)}, u32[]{:S(2)}) copy-start(s32[16]{0:T(128)} %len_ref.1) | copy-start | bytes 196
  26.7 19.3 %copy-start = (bf16[16,128,128]{2,1,0:T(8,128)(2,1)S(1)}, bf16[16,128,128]{2,1,0:T(8,128)(2,1)}, u32[]{:S(2)}) copy-start(bf16[16,128,128]{2,1,0:T(8,128)(2,1)} %cv_ref.1) | copy-start | bytes 1572868

commit v6 on v5

--- a/solution.py
+++ b/solution.py
@@ -39,10 +39,17 @@
 
 
 def pack_kernel(owner_hbm, pages_hbm, out_hbm, owner_ref, pages_ref, wide_ref, out_ref, sems):
-    fetch_pages = pltpu.make_async_copy(pages_hbm, pages_ref, sems.at[0])
+    half = PAGES * KV_HEADS
+    fetch_pages = [
+        pltpu.make_async_copy(
+            pages_hbm.at[pl.ds(half * i, half)], pages_ref.at[pl.ds(half * i, half)], sems.at[3 * i]
+        )
+        for i in range(2)
+    ]
     fetch_owners = pltpu.make_async_copy(owner_hbm, owner_ref, sems.at[1])
     fetch_owners.start()
-    fetch_pages.start()
+    fetch_pages[0].start()
+    fetch_pages[1].start(priority=1)
     start = lax.axis_index("pool") * PAGES
     row, lane = start // 128, lax.rem(start, 128)
     shift = lax.rem(128 - lane, 128)
@@ -62,8 +69,9 @@
         lanes < PAGES, key, jnp.where(lanes < 2 * PAGES, pltpu.roll(key, PAGES, 1) + 1, -1)
     )
     slots = jnp.where(iota((2 * SLOTS, 128), 0) == target[0:1], 1.0, 0.0).astype(jnp.bfloat16)
-    fetch_pages.wait()
-    wide_ref[...] = pages_ref[...].astype(jnp.float32)
+    for i in range(2):
+        fetch_pages[i].wait()
+        wide_ref[pl.ds(half * i, half), :] = pages_ref[pl.ds(half * i, half), :].astype(jnp.float32)
     zeros = jnp.zeros((128 - 2 * PAGES, 128), jnp.bfloat16)
     first_half = iota((POOL // 2, 8, 128), 1) < 4
     stores = []
@@ -94,7 +102,7 @@
         out_ref[:, 0, rows, :] = jnp.concatenate(low, axis=1).astype(jnp.bfloat16)
         out_ref[:, 1, rows, :] = jnp.concatenate(high, axis=1).astype(jnp.bfloat16)
         stores.append(
-            pltpu.make_async_copy(out_ref.at[:, :, rows], out_hbm.at[:, :, rows], sems.at[2 + part])
+            pltpu.make_async_copy(out_ref.at[:, :, rows], out_hbm.at[:, :, rows], sems.at[4 + part])
         )
         stores[-1].start()
     for store in stores:
@@ -112,7 +120,7 @@
             pltpu.VMEM((PAGES * 2 * KV_HEADS, 128), jnp.bfloat16),
             pltpu.VMEM((PAGES * 2 * KV_HEADS, 128), jnp.float32),
             pltpu.VMEM((POOL // 2, 2, 4 * KV_HEADS, 128), jnp.bfloat16),
-            pltpu.SemaphoreType.DMA((4,)),
+            pltpu.SemaphoreType.DMA((6,)),
         ],
         name="pack",
     )(owners, pages)

time: 47.7 us -> 47.7 us (level)
  no operation moved by 1% of the time
where the time goes in v6:
time: 47.7 us; the launch traced here: 47.4 us
  starting transfers between devices  22.2 us (47%)
  waiting for transfers between devices  17.5 us (37%)
  Pallas kernels  4.63 us (10%)
  local copies, waits for them, and re-layouts  2.34 us (5%)
  other arithmetic  0.59 us (1%)
    all_to_all x1, starting transfers between devices, body(): lax.all_to_all(sent.reshape(TENSOR * POOL, 2 * CAP, 128), ('pool', 'tenso...  22.2 us
    all_to_all x1, waiting for transfers between devices, body(): lax.all_to_all(sent.reshape(TENSOR * POOL, 2 * CAP, 128), ('pool', 'tenso...  17.5 us
    pallas_call x1, Pallas kernels, pack(): pl.pallas_call(pack_kernel, out_shape=jax.ShapeDtypeStruct((POOL // 2, 2,...  2.11 us
    pallas_call x1, Pallas kernels, merge(): pl.pallas_call(merge_kernel, out_shape=jax.ShapeDtypeStruct((2, ROWS, GRO...  1.47 us
    pallas_call x1, Pallas kernels, resident(): pl.pallas_call(resident_kernel, out_shape=(jax.ShapeDtypeStruct((QUERIES,...  1.05 us
  transfers between devices with their start and end apart: 1, of which 1 were waited for; matrix products, arithmetic and copies ran while one was open for 4% of the time, Pallas kernels for 2%

profile of v6, /device:TPU:1, one launch (start us, length us, event | category | flops | bytes accessed | tf_op | source)
XLA Modules:
  0.0 47.4 jit_solution(5934869839515772058)
XLA Ops:
  0.0 2.1 %pack.1 = bf16[32,2,32,128]{3,2,1,0:T(8,128)(2,1)} custom-call(s32[24,128]{1,0:T(8,128)} %bitcast.19, bf16[768,128]{1,0:T(8,128)(2,1)} %bitcast.16), custom_call_target="tpu_custom_call" | custom-call | tf_op jit(solution)/shard_map/pack/pallas_call | solution.py:113
  2.1 0.0 copy-start.7
  2.1 0.0 copy-start.8
  2.1 22.2 %all-to-all-start = ((bf16[512,4,128]{2,1,0:T(4,128)(2,1)}), bf16[512,4,128]{2,1,0:T(4,128)(2,1)S(1)}, u32[]{:S(2)}, u32[]{:S(2)}) async-start(bf16[512,4,128]{2,1,0:T(4,128)(2,1)} %bitcast.15), calls=%async_computation | async-start | bytes 1048576 | tf_op jit(solution)/shard_map/all_to_all | solution.py:260
  24.3 0.0 copy-done.7
  24.3 0.0 copy-done.8
  24.4 0.0 copy-start.6
  24.4 0.1 reshape.53
  24.4 0.6 %copy-done.6 = s32[3072]{0:T(1024)S(1)} copy-done((s32[3072]{0:T(1024)S(1)}, s32[3072]{0:T(1024)}, u32[]{:S(2)}) %copy-start.6) | copy-done | bytes 12312
  25.1 0.1 eq.31
  25.2 0.1 select_reduce_fusion.3
  25.3 0.2 select_reduce_fusion.2
  25.5 0.0 copy-start.1
  25.5 0.1 stack.10
  25.6 0.1 copy.23
  25.7 0.1 stack.9
  25.8 0.1 copy.22
  25.9 0.1 copy.29
  26.1 0.2 add_compare_fusion
  26.3 0.2 gt.18
  26.5 0.0 copy-start.2
  26.5 0.0 copy-start.3
  26.5 0.0 copy-start.4
  26.5 0.0 copy-start.5
  26.5 0.1 copy.28
  26.7 0.0 copy-start
  26.7 0.1 broadcast_in_dim.37
  26.8 0.3 broadcast_in_dim.38
  27.1 0.0 copy-done.1
  27.1 0.2 copy-done.2
  27.3 0.0 copy-done.3
  27.4 0.0 copy-done.4
  27.4 0.0 copy-done.5
  27.4 1.1 %resident.1 = (bf16[256,128]{1,0:T(8,128)(2,1)S(1)}, f32[256,256]{1,0:T(8,128)S(1)}, f32[256,128]{1,0:T(8,128)S(1)}, bf16[128,128]{1,0:T(8,128)(2,1)S(1)}) custom-call(s32[16]{0:T(128)S(1)} %copy-done.5, bf16[2,16,1024]{2,1,0:T(8,128)(2,1)S(1)} %copy-done.2, bf16[16,128,128]{2,1,0:T(8,128)(2,1)S(1)} %copy-done.1, bf16[2,16,128]{2,1,0:T(8,128)(2,1)S(1)} %copy-done.3, ...), custom_call_target="tpu_custom_call" | custom-call | flops 10000000 | bytes 1000000 | tf_op jit(solution)/shard_map/resident/pallas_call | solution.py:159
  28.4 17.5 %all-to-all-done = bf16[512,4,128]{2,1,0:T(4,128)(2,1)S(1)} async-done(((bf16[512,4,128]{2,1,0:T(4,128)(2,1)}), bf16[512,4,128]{2,1,0:T(4,128)(2,1)S(1)}, u32[]{:S(2)}, u32[]{:S(2)}) %all-to-all-start) | async-done | bytes 524320 | tf_op jit(solution)/shard_map/all_to_all | solution.py:260
  45.9 0.0 copy-done
  45.9 1.5 %merge.1 = bf16[2,16,1024]{2,1,0:T(8,128)(2,1)} custom-call(f32[2,1024]{1,0:T(2,128)S(1)} %and_select_fusion.bias_ref, bf16[2048,128]{1,0:T(8,128)(2,1)S(1)} %bitcast.14, bf16[256,128]{1,0:T(8,128)(2,1)S(1)} %get-tuple-element.15.q_ref, f32[256,256]{1,0:T(8,128)S(1)} %get-tuple-element.16.score_ref, f32[256,128]{1,0:T(8,128)S(1)} %get-tuple-element.17.m_ref, ...), custom_call_target="tpu_custom_call" | custom-call | tf_op jit(solution)/shard_map/merge/pallas_call | solution.py:218
  (6 shorter events, 0.0 us)
Async XLA Ops:
  2.1 22.2 %copy-start.7 = (s32[3072]{0:T(1024)S(1)}, s32[3072]{0:T(1024)}, u32[]{:S(2)}) copy-start(s32[3072]{0:T(1024)} %param.19) | copy-start | bytes 36868
  2.1 22.2 %copy-start.8 = (s32[3072]{0:T(1024)S(1)}, s32[3072]{0:T(1024)}, u32[]{:S(2)}) copy-start(s32[3072]{0:T(1024)} %param.18) | copy-start | bytes 36868
  2.1 43.8 %all-to-all-start = ((bf16[512,4,128]{2,1,0:T(4,128)(2,1)}), bf16[512,4,128]{2,1,0:T(4,128)(2,1)S(1)}, u32[]{:S(2)}, u32[]{:S(2)}) async-start(bf16[512,4,128]{2,1,0:T(4,128)(2,1)} %bitcast.15), calls=%async_computation | async-start | bytes 1048576 | tf_op jit(solution)/shard_map/all_to_all | solution.py:260
  24.4 0.7 %copy-start.6 = (s32[3072]{0:T(1024)S(1)}, s32[3072]{0:T(1024)}, u32[]{:S(2)}) copy-start(s32[3072]{0:T(1024)} %param.17) | copy-start | bytes 36868
  25.5 1.6 %copy-start.1 = (bf16[16,128,128]{2,1,0:T(8,128)(2,1)S(1)}, bf16[16,128,128]{2,1,0:T(8,128)(2,1)}, u32[]{:S(2)}) copy-start(bf16[16,128,128]{2,1,0:T(8,128)(2,1)} %ck_ref.1) | copy-start | bytes 1572868
  26.5 0.8 %copy-start.2 = (bf16[2,16,1024]{2,1,0:T(8,128)(2,1)S(1)}, bf16[2,16,1024]{2,1,0:T(8,128)(2,1)}, u32[]{:S(2)}) copy-start(bf16[2,16,1024]{2,1,0:T(8,128)(2,1)} %q_ref.1) | copy-start | bytes 196612
  26.5 0.8 %copy-start.3 = (bf16[2,16,128]{2,1,0:T(8,128)(2,1)S(1)}, bf16[2,16,128]{2,1,0:T(8,128)(2,1)}, u32[]{:S(2)}) copy-start(bf16[2,16,128]{2,1,0:T(8,128)(2,1)} %nk_ref.1) | copy-start | bytes 24580
  26.5 0.8 %copy-start.4 = (bf16[2,16,128]{2,1,0:T(8,128)(2,1)S(1)}, bf16[2,16,128]{2,1,0:T(8,128)(2,1)}, u32[]{:S(2)}) copy-start(bf16[2,16,128]{2,1,0:T(8,128)(2,1)} %nv_ref.1) | copy-start | bytes 24580
  26.5 0.8 %copy-start.5 = (s32[16]{0:T(128)S(1)}, s32[16]{0:T(128)}, u32[]{:S(2)}) copy-start(s32[16]{0:T(128)} %len_ref.1) | copy-start | bytes 196
  26.7 19.3 %copy-start = (bf16[16,128,128]{2,1,0:T(8,128)(2,1)S(1)}, bf16[16,128,128]{2,1,0:T(8,128)(2,1)}, u32[]{:S(2)}) copy-start(bf16[16,128,128]{2,1,0:T(8,128)(2,1)} %cv_ref.1) | copy-start | bytes 1572868

commit v7 on v6

--- a/solution.py
+++ b/solution.py
@@ -192,6 +192,11 @@
     tiles = [jnp.exp2(tile - peak) for tile in tiles + [score_ref[:, 0:128], score_ref[:, 128:256]]]
     total = jnp.sum(functools.reduce(jnp.add, tiles), axis=1, keepdims=True)
     tiles = [tile.astype(jnp.bfloat16) for tile in tiles]
+    acc = jnp.dot(
+        jnp.concatenate(tiles[:8] + tiles[9:], axis=1),
+        jnp.concatenate([values, fresh_ref[...]], axis=0),
+        preferred_element_type=jnp.float32,
+    )
     held = []
     for r in range(0, ROWS, 2):
         both = jnp.dot(
@@ -201,11 +206,6 @@
         )
         held += [both[0:16, 0:128], both[16:32, 128:256]]
     held = jnp.concatenate(held, axis=0)
-    acc = jnp.dot(
-        jnp.concatenate(tiles[:8] + tiles[9:], axis=1),
-        jnp.concatenate([values, fresh_ref[...]], axis=0),
-        preferred_element_type=jnp.float32,
-    )
     turn_ref[...] = (acc + held) / total
     for step in range(2):
         for g in range(GROUP):

time: 47.7 us -> 47.7 us (level)
  no operation moved by 1% of the time
where the time goes in v7:
time: 47.7 us; the launch traced here: 47.4 us
  starting transfers between devices  22.2 us (47%)
  waiting for transfers between devices  17.5 us (37%)
  Pallas kernels  4.63 us (10%)
  local copies, waits for them, and re-layouts  2.34 us (5%)
  other arithmetic  0.59 us (1%)
    all_to_all x1, starting transfers between devices, body(): lax.all_to_all(sent.reshape(TENSOR * POOL, 2 * CAP, 128), ('pool', 'tenso...  22.2 us
    all_to_all x1, waiting for transfers between devices, body(): lax.all_to_all(sent.reshape(TENSOR * POOL, 2 * CAP, 128), ('pool', 'tenso...  17.5 us
    pallas_call x1, Pallas kernels, pack(): pl.pallas_call(pack_kernel, out_shape=jax.ShapeDtypeStruct((POOL // 2, 2,...  2.11 us
    pallas_call x1, Pallas kernels, merge(): pl.pallas_call(merge_kernel, out_shape=jax.ShapeDtypeStruct((2, ROWS, GRO...  1.47 us
    pallas_call x1, Pallas kernels, resident(): pl.pallas_call(resident_kernel, out_shape=(jax.ShapeDtypeStruct((QUERIES,...  1.05 us
  transfers between devices with their start and end apart: 1, of which 1 were waited for; matrix products, arithmetic and copies ran while one was open for 4% of the time, Pallas kernels for 2%

profile of v7, /device:TPU:1, one launch (start us, length us, event | category | flops | bytes accessed | tf_op | source)
XLA Modules:
  0.0 47.4 jit_solution(5934869839515772058)
XLA Ops:
  0.0 2.1 %pack.1 = bf16[32,2,32,128]{3,2,1,0:T(8,128)(2,1)} custom-call(s32[24,128]{1,0:T(8,128)} %bitcast.19, bf16[768,128]{1,0:T(8,128)(2,1)} %bitcast.16), custom_call_target="tpu_custom_call" | custom-call | tf_op jit(solution)/shard_map/pack/pallas_call | solution.py:113
  2.1 0.0 copy-start.7
  2.1 0.0 copy-start.8
  2.1 22.2 %all-to-all-start = ((bf16[512,4,128]{2,1,0:T(4,128)(2,1)}), bf16[512,4,128]{2,1,0:T(4,128)(2,1)S(1)}, u32[]{:S(2)}, u32[]{:S(2)}) async-start(bf16[512,4,128]{2,1,0:T(4,128)(2,1)} %bitcast.15), calls=%async_computation | async-start | bytes 1048576 | tf_op jit(solution)/shard_map/all_to_all | solution.py:260
  24.3 0.0 copy-done.7
  24.3 0.0 copy-done.8
  24.4 0.0 copy-start.6
  24.4 0.1 reshape.53
  24.4 0.6 %copy-done.6 = s32[3072]{0:T(1024)S(1)} copy-done((s32[3072]{0:T(1024)S(1)}, s32[3072]{0:T(1024)}, u32[]{:S(2)}) %copy-start.6) | copy-done | bytes 12312
  25.1 0.1 eq.31
  25.2 0.1 select_reduce_fusion.3
  25.3 0.2 select_reduce_fusion.2
  25.5 0.0 copy-start.1
  25.5 0.1 stack.10
  25.6 0.1 copy.23
  25.7 0.1 stack.9
  25.8 0.1 copy.22
  25.9 0.1 copy.29
  26.1 0.2 add_compare_fusion
  26.3 0.2 gt.18
  26.5 0.0 copy-start.2
  26.5 0.0 copy-start.3
  26.5 0.0 copy-start.4
  26.5 0.0 copy-start.5
  26.5 0.1 copy.28
  26.7 0.0 copy-start
  26.7 0.1 broadcast_in_dim.37
  26.8 0.3 broadcast_in_dim.38
  27.1 0.0 copy-done.1
  27.1 0.2 copy-done.2
  27.3 0.0 copy-done.3
  27.4 0.0 copy-done.4
  27.4 0.0 copy-done.5
  27.4 1.1 %resident.1 = (bf16[256,128]{1,0:T(8,128)(2,1)S(1)}, f32[256,256]{1,0:T(8,128)S(1)}, f32[256,128]{1,0:T(8,128)S(1)}, bf16[128,128]{1,0:T(8,128)(2,1)S(1)}) custom-call(s32[16]{0:T(128)S(1)} %copy-done.5, bf16[2,16,1024]{2,1,0:T(8,128)(2,1)S(1)} %copy-done.2, bf16[16,128,128]{2,1,0:T(8,128)(2,1)S(1)} %copy-done.1, bf16[2,16,128]{2,1,0:T(8,128)(2,1)S(1)} %copy-done.3, ...), custom_call_target="tpu_custom_call" | custom-call | flops 10000000 | bytes 1000000 | tf_op jit(solution)/shard_map/resident/pallas_call | solution.py:159
  28.4 17.5 %all-to-all-done = bf16[512,4,128]{2,1,0:T(4,128)(2,1)S(1)} async-done(((bf16[512,4,128]{2,1,0:T(4,128)(2,1)}), bf16[512,4,128]{2,1,0:T(4,128)(2,1)S(1)}, u32[]{:S(2)}, u32[]{:S(2)}) %all-to-all-start) | async-done | bytes 524320 | tf_op jit(solution)/shard_map/all_to_all | solution.py:260
  45.9 0.0 copy-done
  45.9 1.5 %merge.1 = bf16[2,16,1024]{2,1,0:T(8,128)(2,1)} custom-call(f32[2,1024]{1,0:T(2,128)S(1)} %and_select_fusion.bias_ref, bf16[2048,128]{1,0:T(8,128)(2,1)S(1)} %bitcast.14, bf16[256,128]{1,0:T(8,128)(2,1)S(1)} %get-tuple-element.15.q_ref, f32[256,256]{1,0:T(8,128)S(1)} %get-tuple-element.16.score_ref, f32[256,128]{1,0:T(8,128)S(1)} %get-tuple-element.17.m_ref, ...), custom_call_target="tpu_custom_call" | custom-call | tf_op jit(solution)/shard_map/merge/pallas_call | solution.py:218
  (6 shorter events, 0.0 us)
Async XLA Ops:
  2.1 22.2 %copy-start.7 = (s32[3072]{0:T(1024)S(1)}, s32[3072]{0:T(1024)}, u32[]{:S(2)}) copy-start(s32[3072]{0:T(1024)} %param.19) | copy-start | bytes 36868
  2.1 22.2 %copy-start.8 = (s32[3072]{0:T(1024)S(1)}, s32[3072]{0:T(1024)}, u32[]{:S(2)}) copy-start(s32[3072]{0:T(1024)} %param.18) | copy-start | bytes 36868
  2.1 43.8 %all-to-all-start = ((bf16[512,4,128]{2,1,0:T(4,128)(2,1)}), bf16[512,4,128]{2,1,0:T(4,128)(2,1)S(1)}, u32[]{:S(2)}, u32[]{:S(2)}) async-start(bf16[512,4,128]{2,1,0:T(4,128)(2,1)} %bitcast.15), calls=%async_computation | async-start | bytes 1048576 | tf_op jit(solution)/shard_map/all_to_all | solution.py:260
  24.4 0.7 %copy-start.6 = (s32[3072]{0:T(1024)S(1)}, s32[3072]{0:T(1024)}, u32[]{:S(2)}) copy-start(s32[3072]{0:T(1024)} %param.17) | copy-start | bytes 36868
  25.5 1.6 %copy-start.1 = (bf16[16,128,128]{2,1,0:T(8,128)(2,1)S(1)}, bf16[16,128,128]{2,1,0:T(8,128)(2,1)}, u32[]{:S(2)}) copy-start(bf16[16,128,128]{2,1,0:T(8,128)(2,1)} %ck_ref.1) | copy-start | bytes 1572868
  26.5 0.8 %copy-start.2 = (bf16[2,16,1024]{2,1,0:T(8,128)(2,1)S(1)}, bf16[2,16,1024]{2,1,0:T(8,128)(2,1)}, u32[]{:S(2)}) copy-start(bf16[2,16,1024]{2,1,0:T(8,128)(2,1)} %q_ref.1) | copy-start | bytes 196612
  26.5 0.8 %copy-start.3 = (bf16[2,16,128]{2,1,0:T(8,128)(2,1)S(1)}, bf16[2,16,128]{2,1,0:T(8,128)(2,1)}, u32[]{:S(2)}) copy-start(bf16[2,16,128]{2,1,0:T(8,128)(2,1)} %nk_ref.1) | copy-start | bytes 24580
  26.5 0.8 %copy-start.4 = (bf16[2,16,128]{2,1,0:T(8,128)(2,1)S(1)}, bf16[2,16,128]{2,1,0:T(8,128)(2,1)}, u32[]{:S(2)}) copy-start(bf16[2,16,128]{2,1,0:T(8,128)(2,1)} %nv_ref.1) | copy-start | bytes 24580
  26.5 0.8 %copy-start.5 = (s32[16]{0:T(128)S(1)}, s32[16]{0:T(128)}, u32[]{:S(2)}) copy-start(s32[16]{0:T(128)} %len_ref.1) | copy-start | bytes 196
  26.7 19.3 %copy-start = (bf16[16,128,128]{2,1,0:T(8,128)(2,1)S(1)}, bf16[16,128,128]{2,1,0:T(8,128)(2,1)}, u32[]{:S(2)}) copy-start(bf16[16,128,128]{2,1,0:T(8,128)(2,1)} %cv_ref.1) | copy-start | bytes 1572868
